TPU v7x, 32 devices: a whole 2x2x4 slice. The times are simulated.
32 devices in a mesh: dp: 2 (over y), gz: 4 (over x, core), gy: 4 (over z).
Axes of the slice: x: 2, y: 2, z: 4, core: 2. Of those that a mesh axis runs over, the one named last changes fastest.
Arguments:
- volume: bfloat16 [2, 32, 32, 64, 256], P('dp', None, 'gz', 'gy'), may hold values from -6 to 6
- kernel_mid: bfloat16 [64, 32, 3, 3, 3], replicated, may hold values from -0.21875 to 0.21875
- kernel_deep: bfloat16 [128, 64, 3, 3, 3], replicated, may hold values from -0.15625 to 0.15625
- cotangent: bfloat16 [2, 128, 8, 16, 64], P('dp', None, 'gz', 'gy'), may hold values from -6 to 6
Outputs:
- mid_weight_grad: float32 [64, 32, 3, 3, 3], replicated
- deep_weight_grad: float32 [128, 64, 3, 3, 3], P('gy')
All inputs are finite; a program needn't handle non-finite values.
Results may differ from a plain program's by a relative error of at most 0.0034.
Values may be sent and summed in bfloat16 or wider, within the bound.
No kernel may reach another device: no remote copies, remote signals or barrier semaphores. Data moves between devices by JAX's collectives and lax.ppermute only.
A program may use at most 128 MiB of HBM per device.

v0:
```python
import math

import jax
import jax.numpy as jnp
from jax import lax
from jax.sharding import PartitionSpec as P


def passed_along(block, axis, distance):
    devices = range(lax.axis_size(axis))
    route = [(i - distance, i) for i in devices if i - distance in devices]
    return lax.ppermute(block, axis, route)


def conv_down(inputs, kernel, pads):
    return lax.conv_general_dilated(
        inputs,
        kernel,
        (2, 2, 2),
        pads,
        dimension_numbers=("NCDHW", "OIDHW", "NCDHW"),
        preferred_element_type=jnp.float32,
    )


def kernel_grad(inputs, cot_field, pads):
    return lax.conv_general_dilated(
        inputs,
        cot_field,
        (1, 1, 1),
        pads,
        rhs_dilation=(2, 2, 2),
        dimension_numbers=("CNDHW", "IODHW", "CNDHW"),
        preferred_element_type=jnp.float32,
    )


def input_grad(cot_field, kernel, pads):
    flipped = kernel[:, :, ::-1, ::-1, ::-1]
    return lax.conv_general_dilated(
        cot_field,
        flipped,
        (1, 1, 1),
        pads,
        lhs_dilation=(2, 2, 2),
        dimension_numbers=("NCDHW", "IODHW", "NCDHW"),
        preferred_element_type=jnp.float32,
    )


def silu_slope(value):
    sigma = jax.nn.sigmoid(value)
    return sigma * (1.0 + value * (1.0 - sigma))


def on_device(volume, kernel_mid, kernel_deep, cotangent):
    n_dp = lax.axis_size("dp")
    n_gz = lax.axis_size("gz")
    n_gy = lax.axis_size("gy")
    samples, chans, depth, height, breadth = volume.shape
    count_mid = n_dp * samples * (n_gz * depth // 2) * (n_gy * height // 2) * (breadth // 2)
    count_deep = n_dp * samples * (n_gz * depth // 4) * (n_gy * height // 4) * (breadth // 4)
    below = passed_along(volume[:, :, -1:], "gz", 1)
    extended = jnp.concatenate([below, volume], axis=2)
    beside = passed_along(extended[:, :, :, -1:], "gy", 1)
    extended = jnp.concatenate([beside, extended], axis=3)
    pre_mid = conv_down(extended, kernel_mid, ((0, 0), (0, 0), (1, 0)))
    active = jax.nn.silu(pre_mid).astype(jnp.bfloat16)
    rows_all = lax.all_gather(active, "gy", axis=3, tiled=True)
    rows_below = passed_along(rows_all[:, :, -1:], "gz", 1)
    rows_ext = jnp.concatenate([rows_below, rows_all], axis=2)
    share = kernel_deep.shape[0] // n_gy
    own_kernel = lax.dynamic_slice_in_dim(kernel_deep, lax.axis_index("gy") * share, share, 0)
    own_cot = lax.all_to_all(cotangent, "gy", split_axis=1, concat_axis=3, tiled=True)
    deep_part = kernel_grad(rows_ext, own_cot, ((0, 0), (1, 0), (1, 0)))
    back_rows = input_grad(own_cot, own_kernel, ((2, 2), (1, 2), (1, 2)))
    back = lax.psum_scatter(back_rows, "gy", scatter_dimension=3, tiled=True)
    returned = passed_along(back[:, :, :1], "gz", -1)
    back = back[:, :, 1:]
    back = back.at[:, :, -1:].add(returned)
    pre_grad = (back * silu_slope(pre_mid)).astype(jnp.bfloat16)
    mid_part = kernel_grad(extended, pre_grad, ((0, 0), (0, 0), (1, 0)))
    mid_sum = lax.psum(mid_part, ("dp", "gz", "gy"))
    deep_sum = lax.psum(deep_part, ("dp", "gz"))
    return (mid_sum / math.sqrt(count_mid), deep_sum / math.sqrt(count_deep))


def solution(mesh):
    in_specs = (P("dp", None, "gz", "gy", None), P(), P(), P("dp", None, "gz", "gy", None))
    out_specs = (P(), P("gy", None, None, None, None))
    return jax.shard_map(
        on_device, mesh=mesh, in_specs=in_specs, out_specs=out_specs, check_vma=False
    )
```

profile of v0, /device:TPU:0, one launch (start us, length us, event | category | flops | bytes accessed | tf_op | source)
XLA Modules:
  0.0 728.9 jit_solution(5792255726154186664)
XLA Ops:
  7.2 0.0 copy-start
  7.2 0.0 all-gather.2.cloned.1.call-start
  7.2 1.0 slice.50
  8.2 2.4 collective-permute-start
  10.6 1.1 collective-permute-done
  11.8 1.8 constant_dynamic-update-slice_fusion
  13.6 0.3 slice.61
  13.9 4.3 collective-permute-start.1
  18.2 20.4 %copy.67 = bf16[1,32,9,16,256]{1,0,4,3,2:T(2,128)(2,1)} copy(bf16[1,32,9,16,256]{4,3,2,1,0:T(8,128)(2,1)S(1)} %constant_dynamic-update-slice_fusion) | data formatting | bytes 4718592 | tf_op jit(solution)/shard_map/concatenate | solution.py:64
  38.6 0.0 collective-permute-done.1
  38.7 1.3 copy.66
  40.0 36.5 %pad_maximum_fusion = bf16[1,32,9,17,256]{1,0,4,3,2:T(2,128)(2,1)} fusion(bf16[1,32,9,16,256]{1,0,4,3,2:T(2,128)(2,1)} %copy.67, bf16[1,32,9,1,256]{1,0,4,3,2:T(2,128)(2,1)S(1)} %copy.66), kind=kLoop, calls=%fused_computation.2 | loop fusion | flops 1253376 | bytes 5013504 | tf_op jit(solution)/shard_map/concatenate | solution.py:66
  76.5 39.5 %copy.76 = bf16[1,32,9,17,256]{4,1,3,2,0:T(8,128)(2,1)S(1)} copy(bf16[1,32,9,17,256]{1,0,4,3,2:T(2,128)(2,1)} %pad_maximum_fusion) | data formatting | bytes 5013504 | tf_op jit(solution)/shard_map/concatenate | solution.py:66
  116.0 3.6 pad.4
  119.5 14.1 %reshape.54 = bf16[32,9,17,1,8,34]{5,4,0,2,1,3:T(8,128)(2,1)} reshape(bf16[32,9,17,1,272]{4,0,3,2,1:T(8,128)(2,1)} %pad.4) | data formatting | bytes 5326848 | tf_op jit(solution)/shard_map/conv_general_dilated | solution.py:16
  133.6 18.2 %copy.78 = bf16[32,9,17,1,8,34]{0,4,5,2,1,3:T(8,128)(2,1)} copy(bf16[32,9,17,1,8,34]{5,4,0,2,1,3:T(8,128)(2,1)} %reshape.54) | data formatting | bytes 5326848 | tf_op jit(solution)/shard_map/conv_general_dilated | solution.py:16
  151.9 1.3 slice.67
  153.1 0.0 copy-done.3
  153.2 10.9 %multiply_convert_fusion = (bf16[4,8,8,17,64]{4,2,3,1,0:T(8,128)(2,1)S(1)}, f32[4,8,8,17,64]{4,2,3,1,0:T(8,128)}) fusion(pred[8,17]{0,1:T(8,128)(4,1)S(1)} %copy-done.5, bf16[64,32,3,3,3]{0,1,4,3,2:T(8,128)(2,1)S(1)} %copy-done.3, bf16[32,9,17,1,7,2]{0,4,5,2,1,3:T(8,128)(2,1)S(1)} %slice.67, bf16[32,9,17,1,8,34]{0,4,5,2,1,3:T(8,128)(2,1)} %copy.78), kind=kOutput, calls=%fused_computation.12 | convolution fusion | flops 492541952 | bytes 4582408 | tf_op jit(solution)/shard_map/conv_general_dilated | solution.py:16
  164.0 0.1 copy.81
  164.2 0.1 slice.69
  164.3 0.0 copy-start.2
  164.3 3.5 copy.94
  167.8 0.0 all-gather.2.cloned.1.call-update
  167.8 0.2 copy.68
  168.0 0.9 reshape.71
  168.9 4.0 all-to-all-start
  172.9 0.0 reduce-scatter.2.cloned.1.call-start
  172.9 5.9 all-to-all-done
  178.8 0.2 reshape.72
  179.1 0.4 copy.90
  179.5 0.1 pad.2.clone
  179.6 0.2 copy.73
  179.8 8.5 %broadcast_select_fusion = f32[5,32,8,18,64]{4,2,3,1,0:T(8,128)} fusion(pred[8,18]{0,1:T(8,128)(4,1)S(1)} %copy-done.4, bf16[32,2,16,1,7,1]{0,4,5,2,1,3:T(8,128)(2,1)S(1)} %slice.62, bf16[32,2,16,1,8,9]{0,4,5,2,1,3:T(8,128)(2,1)S(1)} %copy.73, bf16[128,64,3,3,3]{0,1,4,3,2:T(8,128)(2,1)S(1)} %copy-done, s32[]{:T(128)S(6)} %select_n.3), kind=kOutput, calls=%fused_computation.9 | convolution fusion | flops 251461632 | bytes 6502548 | tf_op jit(solution)/shard_map/conv_general_dilated | solution.py:40
  188.4 12.3 %copy.75 = f32[5,32,8,18,64]{4,1,3,2,0:T(8,128)} copy(f32[5,32,8,18,64]{4,2,3,1,0:T(8,128)} %broadcast_select_fusion) | data formatting | bytes 11796480 | tf_op jit(solution)/shard_map/conv_general_dilated | solution.py:40
  200.7 10.0 %slice_bitcast_fusion = f32[1,64,5,32,128]{1,3,4,2,0:T(8,128)} fusion(f32[5,32,1,144,64]{4,1,3,0,2:T(8,128)} %bitcast.38), kind=kLoop, calls=%fused_computation.6 | loop fusion | bytes 10485760 | tf_op jit(solution)/shard_map/conv_general_dilated | solution.py:40
  210.7 0.0 reduce-scatter.2.cloned.1.call-update
  210.8 0.0 all-reduce.5.cloned.1.call-start
  210.8 111.8 %all-gather.2.cloned.1.call-done = bf16[1,64,4,32,128]{1,0,4,3,2:T(2,128)(2,1)} async-done(((bf16[1,64,4,8,128]{1,0,4,3,2:T(2,128)(2,1)}), bf16[1,64,4,32,128]{1,0,4,3,2:T(2,128)(2,1)}) %all-gather.2.cloned.1.call-update) | async-done | bytes 2097168 | tf_op jit(solution)/shard_map/all_gather | solution.py:69
  322.6 1.6 slice-done
  324.2 1.0 copy.83
  325.2 2.8 collective-permute-start.3
  328.0 2.0 copy.86
  330.0 2.1 copy.79
  332.1 0.0 collective-permute-done.3
  332.1 4.4 copy.84
  336.5 164.7 %reduce-scatter.2.cloned.1.call-done = f32[1,64,5,8,128]{1,3,4,2,0:T(8,128)} async-done(((f32[1,64,5,32,128]{1,3,4,2,0:T(8,128)}), f32[1,64,5,8,128]{1,3,4,2,0:T(8,128)}) %reduce-scatter.2.cloned.1.call-update) | async-done | bytes 1310736 | tf_op jit(solution)/shard_map/reduce_scatter | solution.py:77
  501.2 1.9 slice.66
  503.1 1.5 collective-permute-start.2
  504.6 28.7 %fusion.5 = f32[32,64,3,3,3]{1,0,4,3,2:T(8,128)} fusion(bf16[1,32,2,16,64]{1,0,4,3,2:T(2,128)(2,1)} %copy.86, bf16[1,64,4,32,128]{1,0,4,3,2:T(2,128)(2,1)} %all-gather.2.cloned.1.call-done, bf16[1,64,1,32,128]{1,0,4,3,2:T(2,128)(2,1)} %copy.84), kind=kOutput, calls=%fused_computation.8 | convolution fusion | flops 225861632 | bytes 2973696 | tf_op jit(solution)/shard_map/conv_general_dilated | solution.py:27
  533.3 0.0 all-reduce.5.cloned.1.call-update
  533.3 0.0 all-reduce.3.cloned.1.call-start
  533.4 0.0 slice-start.1
  533.4 0.0 collective-permute-done.2
  533.4 1.6 slice-done.1
  535.0 1.1 fusion.18
  536.1 0.2 fusion.8
  536.3 0.0 copy-start.1
  536.3 46.7 %fusion.9 = f32[64,32,3,3,3]{0,1,4,3,2:T(8,128)} fusion(bf16[1,32,9,17,256]{1,0,4,3,2:T(2,128)(2,1)} %pad_maximum_fusion, bf16[1,64,4,8,128]{1,3,4,2,0:T(8,128)(2,1)S(1)} %fusion.8), kind=kOutput, calls=%fused_computation.18 | convolution fusion | flops 451805184 | bytes 3252224 | tf_op jit(solution)/shard_map/conv_general_dilated | solution.py:27
  583.0 0.0 all-reduce.3.cloned.1.call-update
  583.0 6.6 all-reduce.5.cloned.1.call-done
  589.6 1.8 broadcast_multiply_fusion
  591.4 129.2 %all-reduce.3.cloned.1.call-done = f32[64,32,3,3,3]{0,1,4,3,2:T(8,128)} async-done(((f32[64,32,3,3,3]{0,1,4,3,2:T(8,128)}), f32[64,32,3,3,3]{0,1,4,3,2:T(8,128)}) %all-reduce.3.cloned.1.call-update) | async-done | bytes 221200 | tf_op jit(solution)/shard_map/psum | solution.py:83
  720.6 1.8 broadcast_multiply_fusion.1
  (14 shorter events, 0.1 us)
Async XLA Ops:
  7.2 172.7 %copy-start = (bf16[128,64,3,3,3]{0,1,4,3,2:T(8,128)(2,1)S(1)}, bf16[128,64,3,3,3]{0,1,4,3,2:T(8,128)(2,1)}, u32[]{:S(2)}) copy-start(bf16[128,64,3,3,3]{0,1,4,3,2:T(8,128)(2,1)} %param.8) | copy-start | bytes 1327108
  7.2 315.4 %all-gather.2.cloned.1.call-start = ((), (), s32[]{:S(2)}) async-start(), calls=%async_computation.4 | async-start | bytes 10485760 | tf_op jit(solution)/shard_map/all_gather | solution.py:69
  8.2 3.5 collective-permute-start
  13.9 24.7 %collective-permute-start.1 = (bf16[1,32,9,1,256]{4,1,3,2,0:T(8,128)(2,1)S(1)}, bf16[1,32,9,1,256]{4,1,3,2,0:T(8,128)(2,1)S(1)}, u32[]{:S(2)}, u32[]{:S(2)}) collective-permute-start(bf16[1,32,9,1,256]{4,1,3,2,0:T(8,128)(2,1)S(1)} %copy.87), channel_id=1, source_target_pairs={{0,1},{1,2},{2,3},{4,5},{5,6},{6,7},{8,9},{9,10},{10,11},{12,13},{... | collective-permute-start | bytes 442376 | tf_op jit(solution)/shard_map/ppermute | solution.py:12
  133.6 19.5 %copy-start.3 = (bf16[64,32,3,3,3]{0,1,4,3,2:T(8,128)(2,1)S(1)}, bf16[64,32,3,3,3]{0,1,4,3,2:T(8,128)(2,1)}, u32[]{:S(2)}) copy-start(bf16[64,32,3,3,3]{0,1,4,3,2:T(8,128)(2,1)} %param.7) | copy-start | bytes 331780
  133.6 19.5 %copy-start.5 = (pred[8,17]{0,1:T(8,128)(4,1)S(1)}, pred[8,17]{0,1:T(8,128)(4,1)}, u32[]{:S(2)}) copy-start(pred[8,17]{0,1:T(8,128)(4,1)} %constant.59) | copy-start | bytes 412
  164.3 3.5 copy-start.2
  168.9 11.0 %copy-start.4 = (pred[8,18]{0,1:T(8,128)(4,1)S(1)}, pred[8,18]{0,1:T(8,128)(4,1)}, u32[]{:S(2)}) copy-start(pred[8,18]{0,1:T(8,128)(4,1)} %constant.58) | copy-start | bytes 436
  168.9 9.9 %all-to-all-start = ((bf16[4,2,8192]{2,1,0:T(2,128)(2,1)}), bf16[4,2,8192]{2,1,0:T(2,128)(2,1)S(1)}, u32[]{:S(2)}, u32[]{:S(2)}) async-start(bf16[4,2,8192]{2,1,0:T(2,128)(2,1)} %reshape.71), calls=%async_computation | async-start | bytes 262144 | tf_op jit(solution)/shard_map/all_to_all | solution.py:74
  172.9 328.3 %reduce-scatter.2.cloned.1.call-start = ((), (), s32[]{:S(2)}) async-start(), calls=%async_computation.2 | async-start | bytes 13107200 | tf_op jit(solution)/shard_map/reduce_scatter | solution.py:77
  210.8 378.9 %all-reduce.5.cloned.1.call-start = ((), (), s32[]{:S(2)}) async-start(), calls=%async_computation.5 | async-start | bytes 884736 | tf_op jit(solution)/shard_map/psum | solution.py:84
  322.6 1.6 slice-start
  325.2 6.9 collective-permute-start.3
  503.1 30.3 %collective-permute-start.2 = (f32[1,64,1,8,128]{1,3,4,2,0:T(8,128)}, f32[1,64,1,8,128]{1,3,4,2,0:T(8,128)S(1)}, u32[]{:S(2)}, u32[]{:S(2)}) collective-permute-start(f32[1,64,1,8,128]{1,3,4,2,0:T(8,128)} %slice.66), channel_id=1, source_target_pairs={{4,0},{8,4},{12,8},{5,1},{9,5},{13,9},{6,2},{10,6},{14,10},{7,3},{... | collective-permute-start | bytes 786440 | tf_op jit(solution)/shard_map/ppermute | solution.py:12
  533.3 187.2 %all-reduce.3.cloned.1.call-start = ((), (), s32[]{:S(2)}) async-start(), calls=%async_computation.3 | async-start | bytes 884736 | tf_op jit(solution)/shard_map/psum | solution.py:83
  533.4 1.6 slice-start.1
  536.3 186.1 %copy-start.1 = (bf16[128,64,3,3,3]{0,1,4,3,2:T(8,128)(2,1)S(1)}, bf16[128,64,3,3,3]{0,1,4,3,2:T(8,128)(2,1)}, u32[]{:S(2)}) copy-start(bf16[128,64,3,3,3]{0,1,4,3,2:T(8,128)(2,1)} %param.8) | copy-start | bytes 1327108
Sparse Core Ops, SparseCore 0:
  167.9 154.6 all-gather.1
  325.0 176.1 reduce-scatter.1
  533.5 56.1 all-reduce.4
  595.4 125.1 all-reduce.2
where the time goes:
time: 732 us; the launch traced here: 729 us
  waiting for transfers between devices  419 us (57%)
  local copies, waits for them, and re-layouts  144 us (20%)
  matrix products  94.8 us (13%)
  other arithmetic  41.5 us (6%)
  starting transfers between devices  15.1 us (2%)
  between operations  14 us (2%)
    reduce_scatter x1, waiting for transfers between devices, on_device(): back = lax.psum_scatter(back_rows, 'gy', scatter_dimension=3, tiled=True)  165 us
    psum x1, waiting for transfers between devices, on_device(): mid_sum = lax.psum(mid_part, ('dp', 'gz', 'gy'))  129 us
    all_gather x1, waiting for transfers between devices, on_device(): rows_all = lax.all_gather(active, 'gy', axis=3, tiled=True)  112 us
    conv_general_dilated x2, matrix products, kernel_grad(): lax.conv_general_dilated(inputs, cot_field, (1, 1, 1), pads, rhs_dilation...  75.4 us
    concatenate x2, local copies, waits for them, and re-layouts, on_device(): extended = jnp.concatenate([beside, extended], axis=3)  43.1 us
    concatenate x1, other arithmetic, on_device(): extended = jnp.concatenate([beside, extended], axis=3)  36.5 us
    conv_general_dilated x3, local copies, waits for them, and re-layouts, conv_down(): lax.conv_general_dilated(inputs, kernel, (2, 2, 2), pads, dimension_numbe...  33.6 us
    conv_general_dilated x4, local copies, waits for them, and re-layouts, input_grad(): lax.conv_general_dilated(cot_field, flipped, (1, 1, 1), pads, lhs_dilatio...  22.5 us
  transfers between devices with their start and end apart: 9, of which 6 were waited for; matrix products, arithmetic and copies ran while one was open for 19% of the time, Pallas kernels for 0%

commit v1 on v0

v1 whole, which is shorter than its diff:
```python
import functools
import math

import jax
import jax.numpy as jnp
from jax import lax
from jax.experimental import pallas as pl
from jax.experimental.pallas import tpu as pltpu
from jax.sharding import PartitionSpec as P

BF16 = jnp.bfloat16
F32 = jnp.float32
NN = (((1,), (0,)), ((), ()))
NT = (((1,), (1,)), ((), ()))


def dot(a, b, dims=NN):
    return lax.dot_general(a, b, dims, preferred_element_type=F32)


def passed_along(block, axis, distance):
    devices = range(lax.axis_size(axis))
    route = [(i - distance, i) for i in devices if i - distance in devices]
    return lax.ppermute(block, axis, route)


def picking_matrix(breadth):
    half = breadth // 2
    row = lax.broadcasted_iota(jnp.int32, (breadth, 3 * half), 0)
    col = lax.broadcasted_iota(jnp.int32, (breadth, 3 * half), 1)
    offset = (col >= half).astype(jnp.int32) + (col >= 2 * half).astype(jnp.int32)
    lane = col - offset * half
    odd = (lane >= half // 2).astype(jnp.int32)
    cell = 2 * (lane - odd * (half // 2)) + odd
    return jnp.where(row == 2 * cell + offset - 1, 1.0, 0.0).astype(BF16)


def put_rows(dst, start, value):
    dst[start : start + value.shape[0], :] = value


def main_kernel(dims, vol, below, beside, cot, cot_above, cot_beside, km, kd, out, even, odd, picked, pairs, act, back, slope, grad, sums):
    c1, c2, c3, depth, height, breadth, n_plane, n_gy = dims
    mz, my, mx = depth // 2, height // 2, breadth // 2
    dz, dy, dx = mz // 2, my // 2, mx // 2
    pick = picking_matrix(breadth)
    blk = 3 * c1

    def place(layer, row, piece):
        dst, at = (even, layer // 2) if layer % 2 == 0 else (odd, layer // 2)
        for a in range(3):
            dst[row * blk + a * c1 : row * blk + (a + 1) * c1, at * mx : (at + 1) * mx] = piece(a).astype(BF16)

    for layer in range(depth + 1):
        if layer == 0:
            rows = below[...]
        else:
            rows = vol[:, layer - 1].reshape(c1 * height, breadth)
        slot = layer % 2 * 3
        for a in range(3):
            picked[slot + a] = dot(rows, pick[:, a * mx : (a + 1) * mx])
        for y in range(height):
            place(layer, y + 1, lambda a: picked[slot + a, pl.ds(y, c1, stride=height), :])
        rim = dot(beside[layer], pick)
        place(layer, 0, lambda a: rim[:, a * mx : (a + 1) * mx])

    def windows(y):
        rows = slice(2 * y * blk, (2 * y + 3) * blk)
        return [even[rows, : mz * mx], odd[rows, :], even[rows, mx:]]

    for y in range(my):
        pre = dot(km[...], jnp.concatenate(windows(y), axis=0))
        sigma = jax.nn.sigmoid(pre)
        slope[y] = sigma * (1.0 + pre * (1.0 - sigma))
        active = (pre * sigma).astype(BF16)
        for z in range(mz):
            cls = (z % 2) * 2 + y % 2
            at = (z // 2) * dy + y // 2
            act[cls * c2 : (cls + 1) * c2, at * mx : (at + 1) * mx] = active[:, z * mx : (z + 1) * mx]

    zero = jnp.zeros((dx, c3), BF16)
    last = lax.broadcasted_iota(jnp.int32, (dx, c3), 0) == dx - 1
    for z in range(dz + 1):
        for y in range(dy + 1):
            if y == dy:
                here = cot_beside[z]
            elif z == dz:
                here = cot_above[y]
            else:
                here = cot[z, y]
            moved = jnp.where(last, 0.0, pltpu.roll(here.astype(F32), dx - 1, 0)).astype(BF16)
            top = (z * (dy + 1) + y) * mx
            pairs[top : top + dx, :] = jnp.concatenate([zero, here, zero], axis=1)
            pairs[top + dx : top + mx, :] = jnp.concatenate([moved, zero, here], axis=1)

    def shifted(sz, sy, z):
        top = ((z + sz) * (dy + 1) + sy) * mx
        return pairs[top : top + dy * mx, :]

    deep = {}
    span = dy * mx
    for sz in range(2):
        for sy in range(2):
            classes = [(pz, py) for pz in range(2) for py in range(2) if pz >= sz and py >= sy]
            taps = [(0 if sz else 1 + pz, 0 if sy else 1 + py) for pz, py in classes]
            lhs = jnp.concatenate([act[(pz * 2 + py) * c2 : (pz * 2 + py + 1) * c2, :] for pz, py in classes], axis=0)
            filters = jnp.concatenate(
                [jnp.concatenate([kd[(az * 3 + ay) * 3 + ax] for ax in range(3)], axis=1) for az, ay in taps], axis=0
            )
            total = None
            for z in range(dz):
                term = dot(lhs[:, z * span : (z + 1) * span], shifted(sz, sy, z))
                total = term if total is None else total + term
                grads = dot(filters, shifted(sz, sy, z), NT)
                for n, (pz, py) in enumerate(classes):
                    rows = slice((pz * 2 + py) * c2, (pz * 2 + py + 1) * c2)
                    piece = grads[n * c2 : (n + 1) * c2]
                    if sz or sy:
                        piece = piece + back[rows, z * span : (z + 1) * span]
                    back[rows, z * span : (z + 1) * span] = piece
            for n, (az, ay) in enumerate(taps):
                for ax in range(3):
                    deep[(az * 3 + ay) * 3 + ax] = total[n * c2 : (n + 1) * c2, ax * c3 : (ax + 1) * c3]

    for y in range(my):
        for z in range(mz):
            cls = (z % 2) * 2 + y % 2
            at = (z // 2) * dy + y // 2
            value = back[cls * c2 : (cls + 1) * c2, at * mx : (at + 1) * mx] * slope[y, :, z * mx : (z + 1) * mx]
            grad[y, :, z * mx : (z + 1) * mx] = value.astype(BF16)

    mids = []
    for az in range(3):
        total = None
        for y in range(my):
            term = dot(windows(y)[az], grad[y], NT)
            total = term if total is None else total + term
        mids.append(total)
    mid = jnp.concatenate(mids, axis=0)

    share = c3 // n_gy
    slabs = 14
    deep_rows = slabs * share // n_plane
    mid_rows = 448 // n_plane
    chunk = deep_rows + mid_rows

    def spread(value, first, per, gys, offset):
        done = 0
        while done < value.shape[0]:
            k, r = divmod(first + done, per)
            count = min(per - r, value.shape[0] - done)
            for g in gys:
                put_rows(sums, (k * n_gy + g) * chunk + offset + r, value[done : done + count])
            done += count

    for slab in range(slabs):
        second = deep[2 * slab + 1] if 2 * slab + 1 < 27 else jnp.zeros((c2, c3), F32)
        turned = jnp.concatenate([deep[2 * slab], second], axis=0).T
        for g in range(n_gy):
            spread(turned[g * share : (g + 1) * share], slab * share, deep_rows, [g], 0)
    half = mid.shape[0] // 2
    packed = jnp.concatenate([mid[:half], mid[half:]], axis=1)
    packed = jnp.concatenate([packed, jnp.zeros((448 - half, 128), F32)], axis=0)
    spread(packed, 0, mid_rows, range(n_gy), deep_rows)
    out[...] = sums[...].astype(BF16)


def last_kernel(dims, scales, got, mid_out, deep_out):
    n_plane, share, c2, deep_rows, mid_rows = dims
    whole = got[...]
    deep = whole[:, :deep_rows].reshape(n_plane * deep_rows, 128) * scales[1]
    mid = whole[:, deep_rows:].reshape(n_plane * mid_rows, 128) * scales[0]
    for a in range(27):
        deep_out[a] = deep[(a // 2) * share : (a // 2 + 1) * share, (a % 2) * c2 : (a % 2 + 1) * c2]
    mid_out[:432] = mid[:432, :64]
    mid_out[432:] = mid[:432, 64:]


def on_device(volume, kernel_mid, kernel_deep, cotangent):
    n_dp = lax.axis_size("dp")
    n_gz = lax.axis_size("gz")
    n_gy = lax.axis_size("gy")
    samples, c1, depth, height, breadth = volume.shape
    c2, c3 = kernel_mid.shape[0], kernel_deep.shape[0]
    count_mid = n_dp * samples * (n_gz * depth // 2) * (n_gy * height // 2) * (breadth // 2)
    count_deep = n_dp * samples * (n_gz * depth // 4) * (n_gy * height // 4) * (breadth // 4)
    mz, my, mx = depth // 2, height // 2, breadth // 2
    dz, dy, dx = mz // 2, my // 2, mx // 2
    n_plane = n_dp * n_gz
    vol = volume[0]
    cot = cotangent[0].transpose(1, 2, 3, 0)
    below = passed_along(vol[:, -1], "gz", 1)
    cot_above = passed_along(cot[0], "gz", -1)
    edge = jnp.concatenate([below[None, :, -1], vol[:, :, -1].transpose(1, 0, 2)], axis=0)
    beside = passed_along(edge, "gy", 1)
    cot_edge = jnp.concatenate([cot[:, 0], cot_above[None, 0]], axis=0)
    cot_beside = passed_along(cot_edge, "gy", -1)
    km = kernel_mid.transpose(2, 3, 4, 1, 0).reshape(27 * c1, c2).T
    kd = kernel_deep.transpose(2, 3, 4, 1, 0).reshape(27, c2, c3)

    share = c3 // n_gy
    deep_rows = 14 * share // n_plane
    mid_rows = 448 // n_plane
    chunk = deep_rows + mid_rows
    total_rows = n_plane * n_gy * chunk
    rows = 3 * c1 * (height + 1)
    sent = pl.pallas_call(
        functools.partial(main_kernel, (c1, c2, c3, depth, height, breadth, n_plane, n_gy)),
        out_shape=jax.ShapeDtypeStruct((total_rows, 128), BF16),
        in_specs=[pl.BlockSpec(memory_space=pltpu.VMEM)] * 8,
        out_specs=pl.BlockSpec(memory_space=pltpu.VMEM),
        scratch_shapes=[
            pltpu.VMEM((rows, (mz + 1) * mx), BF16),
            pltpu.VMEM((rows, mz * mx), BF16),
            pltpu.VMEM((6, c1 * height, mx), F32),
            pltpu.VMEM(((dz + 1) * (dy + 1) * mx, 3 * c3), BF16),
            pltpu.VMEM((4 * c2, dz * dy * mx), BF16),
            pltpu.VMEM((4 * c2, dz * dy * mx), F32),
            pltpu.VMEM((my, c2, mz * mx), F32),
            pltpu.VMEM((my, c2, mz * mx), BF16),
            pltpu.VMEM((total_rows, 128), F32),
        ],
        compiler_params=pltpu.CompilerParams(vmem_limit_bytes=48 * 1024 * 1024),
    )(vol, below.reshape(c1 * height, breadth), beside, cot, cot_above, cot_beside, km, kd)
    got = lax.all_to_all(sent.reshape(n_plane * n_gy, chunk, 128), ("dp", "gz", "gy"), 0, 0)
    own = jnp.sum(got.astype(F32), axis=0)
    whole = lax.all_gather(own, ("dp", "gz"), axis=0)
    scales = (1.0 / math.sqrt(count_mid), 1.0 / math.sqrt(count_deep))
    mid, deep = pl.pallas_call(
        functools.partial(last_kernel, (n_plane, share, c2, deep_rows, mid_rows), scales),
        out_shape=(jax.ShapeDtypeStruct((27 * c1, c2), F32), jax.ShapeDtypeStruct((27, share, c2), F32)),
        in_specs=[pl.BlockSpec(memory_space=pltpu.VMEM)],
        out_specs=(pl.BlockSpec(memory_space=pltpu.VMEM), pl.BlockSpec(memory_space=pltpu.VMEM)),
        compiler_params=pltpu.CompilerParams(vmem_limit_bytes=24 * 1024 * 1024),
    )(whole)
    mid = mid.reshape(3, 3, 3, c1, c2).transpose(4, 3, 0, 1, 2)
    deep = deep.reshape(3, 3, 3, share, c2).transpose(3, 4, 0, 1, 2)
    return mid, deep


def solution(mesh):
    in_specs = (P("dp", None, "gz", "gy", None), P(), P(), P("dp", None, "gz", "gy", None))
    out_specs = (P(), P("gy", None, None, None, None))
    return jax.shard_map(
        on_device, mesh=mesh, in_specs=in_specs, out_specs=out_specs, check_vma=False
    )
```

time: 732 us -> 74.8 us (0.10)
  waiting for transfers between devices: 419 us -> 5.66 us
  local copies, waits for them, and re-layouts: 144 us -> 4.02 us
  matrix products: 94.8 us -> 0 us
  blocking collectives: 0 us -> 41.1 us
  other arithmetic: 41.5 us -> 1.44 us
  between operations: 14 us -> 0.76 us
  Pallas kernels: 0 us -> 10.7 us
    reduce_scatter x1 -> x0, waiting for transfers between devices: 165 us -> none  [on_device(): back = lax.psum_scatter(back_rows, 'gy', scatter_dimension=3, tiled=True)]
    psum x2 -> x0, waiting for transfers between devices: 136 us -> none  [the longest x1 129 us: on_device(): mid_sum = lax.psum(mid_part, ('dp', 'gz', 'gy'))]
    all_gather x1 -> x0, waiting for transfers between devices: 112 us -> none  [on_device(): rows_all = lax.all_gather(active, 'gy', axis=3, tiled=True)]
    conv_general_dilated x4 -> x0, matrix products: 94.8 us -> none  [the longest x2 75.4 us: kernel_grad(): lax.conv_general_dilated(inputs, cot_field, (1, 1, 1), pads, rhs_dilation...]
    concatenate x4 -> x0, local copies, waits for them, and re-layouts: 65.3 us -> none  [the longest x2 43.1 us: on_device(): extended = jnp.concatenate([beside, extended], axis=3)]
    conv_general_dilated x7 -> x0, local copies, waits for them, and re-layouts: 56.1 us -> none  [the longest x3 33.6 us: conv_down(): lax.conv_general_dilated(inputs, kernel, (2, 2, 2), pads, dimension_numbe...]
    concatenate x1 -> x2, other arithmetic: 36.5 us -> 1.31 us  [the longest x1 0.68 us: on_device(): jnp.concatenate([below[None, :, -1], vol[:, :, -1].transpose(1, 0, 2)], a...]
    all_to_all x0 -> x1, blocking collectives: none -> 31.1 us  [on_device(): lax.all_to_all(sent.reshape(n_plane * n_gy, chunk, 128), ('dp', 'gz', 'gy...]
  transfers between devices with their start and end apart: 9 -> 4, of which waited for: 6 -> 2; matrix products, arithmetic and copies ran while one was open for 19% -> 5% of each run, Pallas kernels for 0% -> 0%
where the time goes in v1:
time: 74.8 us; the launch traced here: 74.5 us
  blocking collectives  41.1 us (55%)
  starting transfers between devices  10.8 us (14%)
  Pallas kernels  10.7 us (14%)
  waiting for transfers between devices  5.66 us (8%)
  local copies, waits for them, and re-layouts  4.02 us (5%)
  other arithmetic  1.44 us (2%)
  between operations  0.76 us (1%)
    all_to_all x1, blocking collectives, on_device(): lax.all_to_all(sent.reshape(n_plane * n_gy, chunk, 128), ('dp', 'gz', 'gy...  31.1 us
    ppermute x4, starting transfers between devices, passed_along(): return lax.ppermute(block, axis, route)  10.8 us
    all_gather x1, blocking collectives, on_device(): whole = lax.all_gather(own, ('dp', 'gz'), axis=0)  9.98 us
    pallas_call x1, Pallas kernels, on_device(): pl.pallas_call(functools.partial(main_kernel, (c1, c2, c3, depth, height,...  9.66 us
    ppermute x4, waiting for transfers between devices, passed_along(): return lax.ppermute(block, axis, route)  5.66 us
    unnamed x9, local copies, waits for them, and re-layouts  2.84 us
  transfers between devices with their start and end apart: 4, of which 2 were waited for; matrix products, arithmetic and copies ran while one was open for 5% of the time, Pallas kernels for 0%

profile of v1, /device:TPU:0, one launch (start us, length us, event | category | flops | bytes accessed | tf_op | source)
XLA Modules:
  0.0 74.5 jit_solution(6049634693453697019)
XLA Ops:
  0.6 0.8 %slice_bitcast_fusion.2 = bf16[4,64,128]{2,1,0:T(8,128)(2,1)S(1)} fusion(bf16[2,4,64,128]{3,2,1,0:T(8,128)(2,1)} %bitcast.41), kind=kLoop, calls=%fused_computation.5 | loop fusion | bytes 131072 | tf_op jit(solution)/shard_map/squeeze | solution.py:193
  1.5 0.0 copy-start.2
  1.5 0.0 copy-start.3
  1.5 1.4 %collective-permute-start.2 = (bf16[4,64,128]{2,1,0:T(8,128)(2,1)S(1)}, bf16[4,64,128]{2,1,0:T(8,128)(2,1)S(1)}, u32[]{:S(2)}, u32[]{:S(2)}) collective-permute-start(bf16[4,64,128]{2,1,0:T(8,128)(2,1)S(1)} %slice_bitcast_fusion.2), channel_id=1, source_target_pairs={{4,0},{8,4},{12,8},{5,1},{9,5},{13,9},{6,2},{10,6},{14,10},{7,3},{... | collective-permute-start | bytes 196616 | tf_op jit(solution)/shard_map/ppermute | solution.py:24
  2.9 0.0 copy-start.1
  2.9 2.8 %copy.15 = bf16[1,32,8,16,256]{4,1,2,3,0:T(8,128)(2,1)S(1)} copy(bf16[1,32,8,16,256]{4,3,2,1,0:T(8,128)(2,1)} %param.4) | data formatting | bytes 4194304 | tf_op args[0]
  5.7 0.0 copy-start
  5.8 3.2 %collective-permute-start = (bf16[32,16,256]{2,0,1:T(8,128)(2,1)S(1)}, bf16[32,16,256]{2,0,1:T(8,128)(2,1)S(1)}, u32[]{:S(2)}, u32[]{:S(2)}) collective-permute-start(bf16[32,16,256]{2,0,1:T(8,128)(2,1)S(1)} %slice_bitcast_fusion), channel_id=1, source_target_pairs={{0,4},{4,8},{8,12},{1,5},{5,9},{9,13},{2,6},{6,10},{10,14},{3,7},{... | collective-permute-start | bytes 786440 | tf_op jit(solution)/shard_map/ppermute | solution.py:24
  9.0 0.0 copy-done.2
  9.0 0.0 collective-permute-done.2.cot_above
  9.0 1.1 %collective-permute-done = bf16[32,16,256]{2,0,1:T(8,128)(2,1)S(1)} collective-permute-done((bf16[32,16,256]{2,0,1:T(8,128)(2,1)S(1)}, bf16[32,16,256]{2,0,1:T(8,128)(2,1)S(1)}, u32[]{:S(2)}, u32[]{:S(2)}) %collective-permute-start) | collective-permute-done | bytes 262176 | tf_op jit(solution)/shard_map/ppermute | solution.py:24
  10.1 0.7 pad_maximum_fusion
  10.8 4.9 %collective-permute-start.1 = (bf16[9,32,256]{2,1,0:T(8,128)(2,1)}, bf16[9,32,256]{2,1,0:T(8,128)(2,1)S(1)}, u32[]{:S(2)}, u32[]{:S(2)}) collective-permute-start(bf16[9,32,256]{2,1,0:T(8,128)(2,1)} %pad_maximum_fusion), channel_id=1, source_target_pairs={{0,1},{1,2},{2,3},{4,5},{5,6},{6,7},{8,9},{9,10},{10,11},{12,13},{... | collective-permute-start | bytes 442376 | tf_op jit(solution)/shard_map/ppermute | solution.py:24
  15.7 0.6 pad_maximum_fusion.1
  16.3 1.3 %collective-permute-start.3 = (bf16[3,64,128]{2,1,0:T(8,128)(2,1)}, bf16[3,64,128]{2,1,0:T(8,128)(2,1)S(1)}, u32[]{:S(2)}, u32[]{:S(2)}) collective-permute-start(bf16[3,64,128]{2,1,0:T(8,128)(2,1)} %pad_maximum_fusion.1), channel_id=1, source_target_pairs={{1,0},{2,1},{3,2},{5,4},{6,5},{7,6},{9,8},{10,9},{11,10},{13,12},{... | collective-permute-start | bytes 147464 | tf_op jit(solution)/shard_map/ppermute | solution.py:24
  17.6 0.0 copy-done.3
  17.6 0.1 copy.11
  17.8 0.2 copy.10
  17.9 4.6 %collective-permute-done.3.cot_beside = bf16[3,64,128]{2,1,0:T(8,128)(2,1)S(1)} collective-permute-done((bf16[3,64,128]{2,1,0:T(8,128)(2,1)}, bf16[3,64,128]{2,1,0:T(8,128)(2,1)S(1)}, u32[]{:S(2)}, u32[]{:S(2)}) %collective-permute-start.3) | collective-permute-done | bytes 49184 | tf_op jit(solution)/shard_map/ppermute | solution.py:24
  22.5 0.0 collective-permute-done.1.beside
  22.5 0.0 copy-done.1
  22.5 0.0 copy-done
  22.5 9.7 %shard_map.59 = bf16[3584,128]{1,0:T(8,128)(2,1)S(1)} custom-call(bf16[32,8,16,256]{3,2,1,0:T(8,128)(2,1)S(1)} %bitcast.35, bf16[512,256]{1,0:T(8,128)(2,1)S(1)} %bitcast.38, bf16[9,32,256]{2,1,0:T(8,128)(2,1)S(1)} %collective-permute-done.1.beside, bf16[2,4,64,128]{3,2,1,0:T(8,128)(2,1)S(1)} %bitcast.43, ...), custom_call_target="tpu_custom_call" | custom-call | tf_op jit(solution)/shard_map/pallas_call | solution.py:207
  32.2 31.1 %all_to_all.5 = bf16[32,112,128]{2,1,0:T(8,128)(2,1)S(1)} all-to-all(bf16[32,112,128]{2,1,0:T(8,128)(2,1)S(1)} %bitcast.36), channel_id=1, replica_groups=mesh['dp'=2,'gz'=4,'gy'=4] {'dp','gz','gy'}, dimensions={0} | all-to-all | bytes 1835008 | tf_op jit(solution)/shard_map/all_to_all | solution.py:225
  63.3 0.1 convert_reduce_fusion
  63.5 10.0 %all-gather = f32[896,128]{1,0:T(8,128)S(1)} all-gather(f32[112,128]{1,0:T(8,128)S(1)} %convert_reduce_fusion), channel_id=2, replica_groups=mesh['dp'=2,'gz'=4,'gy'=4] {'dp','gz'}, dimensions={0}, use_global_device_ids=true | all-gather | bytes 516096 | tf_op jit(solution)/shard_map/all_gather | solution.py:227
  73.4 1.0 %shard_map.60 = (f32[864,64]{1,0:T(8,128)}, f32[27,32,64]{2,1,0:T(8,128)}) custom-call(f32[8,112,128]{2,1,0:T(8,128)S(1)} %bitcast.37), custom_call_target="tpu_custom_call" | custom-call | tf_op jit(solution)/shard_map/pallas_call | solution.py:229
  (5 shorter events, 0.0 us)
Async XLA Ops:
  1.5 7.5 %copy-start.2 = (bf16[1,128,2,4,64]{1,4,3,2,0:T(8,128)(2,1)S(1)}, bf16[1,128,2,4,64]{1,4,3,2,0:T(8,128)(2,1)}, u32[]{:S(2)}) copy-start(bf16[1,128,2,4,64]{1,4,3,2,0:T(8,128)(2,1)} %param.7) | copy-start | bytes 393220
  1.5 16.2 %copy-start.3 = (bf16[64,32,3,3,3]{0,1,4,3,2:T(8,128)(2,1)S(1)}, bf16[64,32,3,3,3]{0,1,4,3,2:T(8,128)(2,1)}, u32[]{:S(2)}) copy-start(bf16[64,32,3,3,3]{0,1,4,3,2:T(8,128)(2,1)} %param.5) | copy-start | bytes 331780
  1.5 7.5 %collective-permute-start.2 = (bf16[4,64,128]{2,1,0:T(8,128)(2,1)S(1)}, bf16[4,64,128]{2,1,0:T(8,128)(2,1)S(1)}, u32[]{:S(2)}, u32[]{:S(2)}) collective-permute-start(bf16[4,64,128]{2,1,0:T(8,128)(2,1)S(1)} %slice_bitcast_fusion.2), channel_id=1, source_target_pairs={{4,0},{8,4},{12,8},{5,1},{9,5},{13,9},{6,2},{10,6},{14,10},{7,3},{... | collective-permute-start | bytes 196616 | tf_op jit(solution)/shard_map/ppermute | solution.py:24
  2.9 19.6 %copy-start.1 = (bf16[128,64,3,3,3]{0,1,4,3,2:T(8,128)(2,1)S(1)}, bf16[128,64,3,3,3]{0,1,4,3,2:T(8,128)(2,1)}, u32[]{:S(2)}) copy-start(bf16[128,64,3,3,3]{0,1,4,3,2:T(8,128)(2,1)} %param.6) | copy-start | bytes 1327108
  5.7 16.8 %copy-start = (bf16[1,32,8,16,256]{4,3,2,1,0:T(8,128)(2,1)S(1)}, bf16[1,32,8,16,256]{4,3,2,1,0:T(8,128)(2,1)}, u32[]{:S(2)}) copy-start(bf16[1,32,8,16,256]{4,3,2,1,0:T(8,128)(2,1)} %param.4) | copy-start | bytes 6291460
  5.8 4.3 %collective-permute-start = (bf16[32,16,256]{2,0,1:T(8,128)(2,1)S(1)}, bf16[32,16,256]{2,0,1:T(8,128)(2,1)S(1)}, u32[]{:S(2)}, u32[]{:S(2)}) collective-permute-start(bf16[32,16,256]{2,0,1:T(8,128)(2,1)S(1)} %slice_bitcast_fusion), channel_id=1, source_target_pairs={{0,4},{4,8},{8,12},{1,5},{5,9},{9,13},{2,6},{6,10},{10,14},{3,7},{... | collective-permute-start | bytes 786440 | tf_op jit(solution)/shard_map/ppermute | solution.py:24
  10.8 11.7 %collective-permute-start.1 = (bf16[9,32,256]{2,1,0:T(8,128)(2,1)}, bf16[9,32,256]{2,1,0:T(8,128)(2,1)S(1)}, u32[]{:S(2)}, u32[]{:S(2)}) collective-permute-start(bf16[9,32,256]{2,1,0:T(8,128)(2,1)} %pad_maximum_fusion), channel_id=1, source_target_pairs={{0,1},{1,2},{2,3},{4,5},{5,6},{6,7},{8,9},{9,10},{10,11},{12,13},{... | collective-permute-start | bytes 442376 | tf_op jit(solution)/shard_map/ppermute | solution.py:24
  16.3 6.2 %collective-permute-start.3 = (bf16[3,64,128]{2,1,0:T(8,128)(2,1)}, bf16[3,64,128]{2,1,0:T(8,128)(2,1)S(1)}, u32[]{:S(2)}, u32[]{:S(2)}) collective-permute-start(bf16[3,64,128]{2,1,0:T(8,128)(2,1)} %pad_maximum_fusion.1), channel_id=1, source_target_pairs={{1,0},{2,1},{3,2},{5,4},{6,5},{7,6},{9,8},{10,9},{11,10},{13,12},{... | collective-permute-start | bytes 147464 | tf_op jit(solution)/shard_map/ppermute | solution.py:24

commit v2 on v1

v2 whole, which is shorter than its diff:
```python
import functools
import math

import jax
import jax.numpy as jnp
from jax import lax
from jax.experimental import pallas as pl
from jax.experimental.pallas import tpu as pltpu
from jax.sharding import Mesh, PartitionSpec as P

BF16 = jnp.bfloat16
F32 = jnp.float32
NN = (((1,), (0,)), ((), ()))
NT = (((1,), (1,)), ((), ()))


def dot(a, b, dims=NN):
    return lax.dot_general(a, b, dims, preferred_element_type=F32)


def passed_along(block, axis, distance):
    devices = range(lax.axis_size(axis))
    route = [(i - distance, i) for i in devices if i - distance in devices]
    return lax.ppermute(block, axis, route)


def picking_matrix(breadth):
    half = breadth // 2
    row = lax.broadcasted_iota(jnp.int32, (breadth, 3 * half), 0)
    col = lax.broadcasted_iota(jnp.int32, (breadth, 3 * half), 1)
    offset = (col >= half).astype(jnp.int32) + (col >= 2 * half).astype(jnp.int32)
    lane = col - offset * half
    odd = (lane >= half // 2).astype(jnp.int32)
    cell = 2 * (lane - odd * (half // 2)) + odd
    return jnp.where(row == 2 * cell + offset - 1, 1.0, 0.0).astype(BF16)


def place(dst, row, lanes, piece):
    c1 = piece(0).shape[0]
    for a in range(3):
        dst[row + a * c1 : row + (a + 1) * c1, lanes] = piece(a).astype(BF16)


def spread_layer(rows, pick, picked, c1, height, mx, put):
    for a in range(3):
        picked[a] = dot(rows, pick[:, a * mx : (a + 1) * mx])
    for y in range(height):
        put(y, lambda a: picked[a, pl.ds(y, c1, stride=height), :])


def edge_kernel(dims, vol, layer, side, tall):
    c1, depth, height, breadth = dims
    layer[...] = vol[:, depth - 1].reshape(c1 * height, breadth)
    side[0] = jnp.zeros((c1, breadth), BF16)
    for z in range(depth):
        top = vol[:, z].astype(F32)[:, height - 8 :].reshape(c1 * 8, breadth)
        for part in range(breadth // 128):
            lanes = slice(part * 128, (part + 1) * 128)
            slot = (z * (breadth // 128) + part) % 4
            tall[slot] = top[:, lanes]
            side[z + 1, :, lanes] = tall[slot, pl.ds(7, c1, stride=8), :].astype(BF16)


def gather_kernel(dims, vol, even, odd, picked):
    c1, depth, height, breadth = dims
    mx = breadth // 2
    pick = picking_matrix(breadth)
    for layer in range(depth):
        rows = vol[:, layer].reshape(c1 * height, breadth)
        dst = even if layer % 2 else odd
        lanes = slice(layer // 2 * mx, (layer // 2 + 1) * mx)
        put = lambda y, piece: place(dst, y * 3 * c1, lanes, piece)
        spread_layer(rows, pick, picked.at[layer % 2], c1, height, mx, put)


def main_kernel(dims, even, odd, below, beside, cot, cot_above, cot_beside, km, kd, me, keep, send, rim_z, rim_even, rim_odd, picked, pairs, act, back, slope, grad, sums):
    c1, c2, c3, depth, height, breadth, n_pl, n_gy = dims
    mz, my, mx = depth // 2, height // 2, breadth // 2
    dz, dy, dx = mz // 2, my // 2, mx // 2
    pick = picking_matrix(breadth)
    blk = 3 * c1

    put = lambda y, piece: place(rim_z, (y + 1) * blk, slice(0, mx), piece)
    spread_layer(below[...], pick, picked, c1, height, mx, put)
    for layer in range(depth + 1):
        rim = dot(beside[layer], pick)
        if layer == 0:
            dst, at = rim_z, 0
        else:
            dst, at = (rim_odd, layer // 2) if layer % 2 else (rim_even, layer // 2 - 1)
        place(dst, 0, slice(at * mx, (at + 1) * mx), lambda a: rim[:, a * mx : (a + 1) * mx])

    def window(y, az):
        source, rim = (odd, rim_odd) if az == 1 else (even, rim_even)
        if y == 0:
            cells = jnp.concatenate([rim[...], source[: 2 * blk, :]], axis=0)
        else:
            cells = source[(2 * y - 1) * blk : (2 * y + 2) * blk, :]
        if az == 0:
            cells = jnp.concatenate([rim_z[2 * y * blk : (2 * y + 3) * blk, :], cells[:, : (mz - 1) * mx]], axis=1)
        return cells

    turned_km = km[...].astype(F32).T.astype(BF16)
    for y in range(my):
        pre = dot(turned_km, jnp.concatenate([window(y, az) for az in range(3)], axis=0))
        sigma = jax.nn.sigmoid(pre)
        slope[y] = sigma * (1.0 + pre * (1.0 - sigma))
        active = (pre * sigma).astype(BF16)
        for z in range(mz):
            cls = (z % 2) * 2 + y % 2
            at = (z // 2) * dy + y // 2
            act[cls * c2 : (cls + 1) * c2, at * mx : (at + 1) * mx] = active[:, z * mx : (z + 1) * mx]

    zero = jnp.zeros((dx, c3), BF16)
    last = lax.broadcasted_iota(jnp.int32, (dx, c3), 0) == dx - 1
    for z in range(dz + 1):
        for y in range(dy + 1):
            if y == dy:
                here = cot_beside[z]
            elif z == dz:
                here = cot_above[y]
            else:
                here = cot[z, y]
            moved = jnp.where(last, 0.0, pltpu.roll(here.astype(F32), dx - 1, 0)).astype(BF16)
            top = (z * (dy + 1) + y) * mx
            pairs[top : top + dx, :] = jnp.concatenate([zero, here, zero], axis=1)
            pairs[top + dx : top + mx, :] = jnp.concatenate([moved, zero, here], axis=1)

    def shifted(sz, sy, z):
        top = ((z + sz) * (dy + 1) + sy) * mx
        return pairs[top : top + dy * mx, :]

    deep = {}
    span = dy * mx
    for sz in range(2):
        for sy in range(2):
            classes = [(pz, py) for pz in range(2) for py in range(2) if pz >= sz and py >= sy]
            taps = [(0 if sz else 1 + pz, 0 if sy else 1 + py) for pz, py in classes]
            lhs = jnp.concatenate([act[(pz * 2 + py) * c2 : (pz * 2 + py + 1) * c2, :] for pz, py in classes], axis=0)
            filters = jnp.concatenate(
                [jnp.concatenate([kd[(az * 3 + ay) * 3 + ax] for ax in range(3)], axis=1) for az, ay in taps], axis=0
            )
            total = None
            for z in range(dz):
                term = dot(lhs[:, z * span : (z + 1) * span], shifted(sz, sy, z))
                total = term if total is None else total + term
                grads = dot(filters, shifted(sz, sy, z), NT)
                for n, (pz, py) in enumerate(classes):
                    rows = slice((pz * 2 + py) * c2, (pz * 2 + py + 1) * c2)
                    piece = grads[n * c2 : (n + 1) * c2]
                    if sz or sy:
                        piece = piece + back[rows, z * span : (z + 1) * span]
                    back[rows, z * span : (z + 1) * span] = piece
            for n, (az, ay) in enumerate(taps):
                for ax in range(3):
                    deep[(az * 3 + ay) * 3 + ax] = total[n * c2 : (n + 1) * c2, ax * c3 : (ax + 1) * c3]

    for y in range(my):
        for z in range(mz):
            cls = (z % 2) * 2 + y % 2
            at = (z // 2) * dy + y // 2
            value = back[cls * c2 : (cls + 1) * c2, at * mx : (at + 1) * mx] * slope[y, :, z * mx : (z + 1) * mx]
            grad[y, :, z * mx : (z + 1) * mx] = value.astype(BF16)

    mids = []
    for az in range(3):
        total = None
        for y in range(my):
            term = dot(window(y, az), grad[y], NT)
            total = term if total is None else total + term
        mids.append(total)
    mid = jnp.concatenate(mids, axis=0)

    share = c3 // n_gy
    per = 448 // (2 * n_pl)
    chunk = (n_gy + 1) * per

    def spread(value, first, offset):
        done = 0
        while done < value.shape[0]:
            k, r = divmod(first + done, per)
            count = min(per - r, value.shape[0] - done)
            core, start = k % 2, k // 2 * chunk + offset + r
            sums[core, start : start + count, :] = value[done : done + count]
            done += count

    for slab in range(14):
        second = deep[2 * slab + 1] if 2 * slab + 1 < 27 else jnp.zeros((c2, c3), F32)
        turned = jnp.concatenate([deep[2 * slab], second], axis=0).T
        for g in range(n_gy):
            spread(turned[g * share : (g + 1) * share], slab * share, g * per)
    half = mid.shape[0] // 2
    packed = jnp.concatenate([mid[:half], mid[half:]], axis=1)
    packed = jnp.concatenate([packed, jnp.zeros((448 - half, 128), F32)], axis=0)
    spread(packed, 0, n_gy * per)
    keep[...] = sums[me[0]]
    send[...] = sums[1 - me[0]]


def last_kernel(dims, scales, got, mid_out, deep_out):
    n_all, share, c2, per = dims
    whole = got[...]
    deep = whole[:, :per].reshape(n_all * per, 128) * scales[1]
    mid = whole[:, per:].reshape(n_all * per, 128) * scales[0]
    for a in range(27):
        deep_out[a] = deep[(a // 2) * share : (a // 2 + 1) * share, (a % 2) * c2 : (a % 2 + 1) * c2]
    mid_out[:432] = mid[:432, :64]
    mid_out[432:] = mid[:432, 64:]


def on_device(volume, kernel_mid, kernel_deep, cotangent):
    n_dp = lax.axis_size("dp")
    gz = ("gx", "core")
    n_gz = lax.axis_size(gz)
    n_gy = lax.axis_size("gy")
    samples, c1, depth, height, breadth = volume.shape
    c2, c3 = kernel_mid.shape[0], kernel_deep.shape[0]
    count_mid = n_dp * samples * (n_gz * depth // 2) * (n_gy * height // 2) * (breadth // 2)
    count_deep = n_dp * samples * (n_gz * depth // 4) * (n_gy * height // 4) * (breadth // 4)
    mz, my, mx = depth // 2, height // 2, breadth // 2
    dz, dy, dx = mz // 2, my // 2, mx // 2
    n_pl = n_dp * n_gz // 2
    vol = volume[0]
    cot = cotangent[0].transpose(1, 2, 3, 0)
    in_vmem = pl.BlockSpec(memory_space=pltpu.VMEM)
    layer, side = pl.pallas_call(
        functools.partial(edge_kernel, (c1, depth, height, breadth)),
        out_shape=(
            jax.ShapeDtypeStruct((c1 * height, breadth), BF16),
            jax.ShapeDtypeStruct((depth + 1, c1, breadth), BF16),
        ),
        in_specs=[in_vmem],
        out_specs=(in_vmem, in_vmem),
        scratch_shapes=[pltpu.VMEM((4, c1 * 8, 128), F32)],
        compiler_params=pltpu.CompilerParams(vmem_limit_bytes=16 * 1024 * 1024),
    )(vol)
    below = passed_along(layer, gz, 1)
    cot_above = passed_along(cot[0], gz, -1)
    edge = side.at[0].set(below.reshape(c1, height, breadth)[:, -1])
    beside = passed_along(edge, "gy", 1)
    cot_edge = jnp.concatenate([cot[:, 0], cot_above[None, 0]], axis=0)
    cot_beside = passed_along(cot_edge, "gy", -1)
    km = kernel_mid.transpose(2, 3, 4, 1, 0).reshape(27 * c1, c2)
    kd = kernel_deep.transpose(2, 3, 4, 1, 0).reshape(27, c2, c3)

    share = c3 // n_gy
    per = 448 // (2 * n_pl)
    chunk = (n_gy + 1) * per
    me = lax.axis_index("core").reshape(1)
    blk = 3 * c1
    own_cells = jax.ShapeDtypeStruct((height * blk, mz * mx), BF16)
    even, odd = pl.pallas_call(
        functools.partial(gather_kernel, (c1, depth, height, breadth)),
        out_shape=(own_cells, own_cells),
        in_specs=[in_vmem],
        out_specs=(in_vmem, in_vmem),
        scratch_shapes=[pltpu.VMEM((2, 3, c1 * height, mx), F32)],
        cost_estimate=pl.CostEstimate(flops=2 * c1 * depth * height * breadth * 3 * mx, bytes_accessed=8 << 20, transcendentals=0),
        compiler_params=pltpu.CompilerParams(vmem_limit_bytes=24 * 1024 * 1024),
    )(vol)
    keep, send = pl.pallas_call(
        functools.partial(main_kernel, (c1, c2, c3, depth, height, breadth, n_pl, n_gy)),
        out_shape=(jax.ShapeDtypeStruct((n_pl * chunk, 128), F32), jax.ShapeDtypeStruct((n_pl * chunk, 128), F32)),
        in_specs=[in_vmem] * 9 + [pl.BlockSpec(memory_space=pltpu.SMEM)],
        out_specs=(in_vmem, in_vmem),
        scratch_shapes=[
            pltpu.VMEM(((height + 1) * blk, mx), BF16),
            pltpu.VMEM((blk, mz * mx), BF16),
            pltpu.VMEM((blk, mz * mx), BF16),
            pltpu.VMEM((3, c1 * height, mx), F32),
            pltpu.VMEM(((dz + 1) * (dy + 1) * mx, 3 * c3), BF16),
            pltpu.VMEM((4 * c2, dz * dy * mx), BF16),
            pltpu.VMEM((4 * c2, dz * dy * mx), F32),
            pltpu.VMEM((my, c2, mz * mx), F32),
            pltpu.VMEM((my, c2, mz * mx), BF16),
            pltpu.VMEM((2, n_pl * chunk, 128), F32),
        ],
        compiler_params=pltpu.CompilerParams(vmem_limit_bytes=48 * 1024 * 1024),
    )(even, odd, below, beside, cot, cot_above, cot_beside, km, kd, me)
    other = lax.ppermute(send, "core", [(0, 1), (1, 0)])
    pair = (keep + other).astype(BF16).reshape(n_pl, chunk, 128)
    own = jnp.sum(lax.all_to_all(pair, ("dp", "gx"), 0, 0).astype(F32), axis=0)
    deep_own = own[: n_gy * per].reshape(n_gy, per, 128)
    mid_own = jnp.broadcast_to(own[n_gy * per :], (n_gy, per, 128))
    column = jnp.concatenate([deep_own, mid_own], axis=1).astype(BF16)
    own = jnp.sum(lax.all_to_all(column, "gy", 0, 0).astype(F32), axis=0)
    whole = lax.all_gather(own, ("dp", "gx", "core"), axis=0)
    scales = (1.0 / math.sqrt(count_mid), 1.0 / math.sqrt(count_deep))
    mid, deep = pl.pallas_call(
        functools.partial(last_kernel, (2 * n_pl, share, c2, per), scales),
        out_shape=(jax.ShapeDtypeStruct((27 * c1, c2), F32), jax.ShapeDtypeStruct((27, share, c2), F32)),
        in_specs=[in_vmem],
        out_specs=(in_vmem, in_vmem),
        compiler_params=pltpu.CompilerParams(vmem_limit_bytes=24 * 1024 * 1024),
    )(whole)
    mid = mid.reshape(3, 3, 3, c1, c2).transpose(4, 3, 0, 1, 2)
    deep = deep.reshape(3, 3, 3, share, c2).transpose(3, 4, 0, 1, 2)
    return mid, deep


def solution(mesh):
    n_dp, n_gz, n_gy = (mesh.shape[name] for name in ("dp", "gz", "gy"))
    split = Mesh(mesh.devices.reshape(n_dp, n_gz // 2, 2, n_gy), ("dp", "gx", "core", "gy"))
    by_cells = P("dp", None, ("gx", "core"), "gy", None)
    in_specs = (by_cells, P(), P(), by_cells)
    out_specs = (P(), P("gy", None, None, None, None))
    return jax.shard_map(
        on_device, mesh=split, in_specs=in_specs, out_specs=out_specs, check_vma=False
    )
```

time: 74.8 us -> 60.9 us (0.81)
  blocking collectives: 41.1 us -> 29.4 us
  local copies, waits for them, and re-layouts: 4.02 us -> 2.52 us
  other arithmetic: 1.44 us -> 0.13 us
  waiting for transfers between devices: 5.66 us -> 6.89 us
    all_to_all x1 -> x2, blocking collectives: 31.1 us -> 20.6 us  [the longest x1 10.3 us: on_device(): own = jnp.sum(lax.all_to_all(column, 'gy', 0, 0).astype(F32), axis=0)]
    pallas_call x1, Pallas kernels: 9.66 us -> 5.92 us  [on_device(): pl.pallas_call(functools.partial(main_kernel, (c1, c2, c3, depth, height,...]
    pallas_call x1 -> x3, Pallas kernels: 1.04 us -> 4.53 us  [the longest x1 3.3 us: on_device(): pl.pallas_call(functools.partial(gather_kernel, (c1, depth, height, bread...]
    ppermute x4, starting transfers between devices: 10.8 us -> 8.7 us  [passed_along(): return lax.ppermute(block, axis, route)]
    ppermute x0 -> x1, waiting for transfers between devices: none -> 1.61 us  [on_device(): other = lax.ppermute(send, 'core', [(0, 1), (1, 0)])]
    ppermute x0 -> x1, starting transfers between devices: none -> 1.57 us  [on_device(): other = lax.ppermute(send, 'core', [(0, 1), (1, 0)])]
    unnamed x9 -> x10, local copies, waits for them, and re-layouts: 2.84 us -> 1.6 us
    all_gather x1, blocking collectives: 9.98 us -> 8.84 us  [on_device(): whole = lax.all_gather(own, ('dp', 'gx', 'core'), axis=0)]
  transfers between devices with their start and end apart: 4 -> 5, of which waited for: 2 -> 3; matrix products, arithmetic and copies ran while one was open for 5% -> 1% of each run, Pallas kernels for 0% -> 5%
where the time goes in v2:
time: 60.9 us; the launch traced here: 60.5 us
  blocking collectives  29.4 us (48%)
  Pallas kernels  10.4 us (17%)
  starting transfers between devices  10.3 us (17%)
  waiting for transfers between devices  6.89 us (11%)
  local copies, waits for them, and re-layouts  2.52 us (4%)
  between operations  0.81 us (1%)
    all_to_all x1, blocking collectives, on_device(): own = jnp.sum(lax.all_to_all(column, 'gy', 0, 0).astype(F32), axis=0)  10.3 us
    all_to_all x1, blocking collectives, on_device(): own = jnp.sum(lax.all_to_all(pair, ('dp', 'gx'), 0, 0).astype(F32), axis=0)  10.2 us
    all_gather x1, blocking collectives, on_device(): whole = lax.all_gather(own, ('dp', 'gx', 'core'), axis=0)  8.84 us
    ppermute x4, starting transfers between devices, passed_along(): return lax.ppermute(block, axis, route)  8.7 us
    pallas_call x1, Pallas kernels, on_device(): pl.pallas_call(functools.partial(main_kernel, (c1, c2, c3, depth, height,...  5.92 us
    ppermute x4, waiting for transfers between devices, passed_along(): return lax.ppermute(block, axis, route)  5.28 us
    pallas_call x1, Pallas kernels, on_device(): pl.pallas_call(functools.partial(gather_kernel, (c1, depth, height, bread...  3.3 us
    ppermute x1, waiting for transfers between devices, on_device(): other = lax.ppermute(send, 'core', [(0, 1), (1, 0)])  1.61 us
  transfers between devices with their start and end apart: 5, of which 3 were waited for; matrix products, arithmetic and copies ran while one was open for 1% of the time, Pallas kernels for 5%

profile of v2, /device:TPU:0, one launch (start us, length us, event | category | flops | bytes accessed | tf_op | source)
XLA Modules:
  0.0 60.5 jit_solution(133539773204384639)
XLA Ops:
  0.6 0.0 copy-start
  0.6 1.6 %copy-done = bf16[1,32,8,16,256]{4,3,2,1,0:T(8,128)(2,1)S(1)} copy-done((bf16[1,32,8,16,256]{4,3,2,1,0:T(8,128)(2,1)S(1)}, bf16[1,32,8,16,256]{4,3,2,1,0:T(8,128)(2,1)}, u32[]{:S(2)}) %copy-start) | copy-done | bytes 2097176
  2.2 0.0 copy-start.3
  2.2 0.0 copy-start.1
  2.2 0.2 shard_map.60
  2.4 2.5 %collective-permute-start = (bf16[512,256]{1,0:T(8,128)(2,1)S(1)}, bf16[512,256]{1,0:T(8,128)(2,1)S(1)}, u32[]{:S(2)}, u32[]{:S(2)}) collective-permute-start(bf16[512,256]{1,0:T(8,128)(2,1)S(1)} %get-tuple-element.24), channel_id=1, source_target_pairs={{0,4},{4,8},{8,12},{1,5},{5,9},{9,13},{2,6},{6,10},{10,14},{3,7},{... | collective-permute-start | bytes 786440 | tf_op jit(solution)/shard_map/ppermute | solution.py:24
  4.9 0.8 %slice_bitcast_fusion = bf16[4,64,128]{2,1,0:T(8,128)(2,1)S(1)} fusion(bf16[2,4,64,128]{3,2,1,0:T(8,128)(2,1)} %bitcast.33), kind=kLoop, calls=%fused_computation.5 | loop fusion | bytes 131072 | tf_op jit(solution)/shard_map/squeeze | solution.py:238
  5.8 1.3 %collective-permute-start.2 = (bf16[4,64,128]{2,1,0:T(8,128)(2,1)S(1)}, bf16[4,64,128]{2,1,0:T(8,128)(2,1)S(1)}, u32[]{:S(2)}, u32[]{:S(2)}) collective-permute-start(bf16[4,64,128]{2,1,0:T(8,128)(2,1)S(1)} %slice_bitcast_fusion), channel_id=1, source_target_pairs={{4,0},{8,4},{12,8},{5,1},{9,5},{13,9},{6,2},{10,6},{14,10},{7,3},{... | collective-permute-start | bytes 196616 | tf_op jit(solution)/shard_map/ppermute | solution.py:24
  7.1 0.0 copy-done.3
  7.1 3.9 %collective-permute-done.2.cot_above = bf16[4,64,128]{2,1,0:T(8,128)(2,1)S(1)} collective-permute-done((bf16[4,64,128]{2,1,0:T(8,128)(2,1)S(1)}, bf16[4,64,128]{2,1,0:T(8,128)(2,1)S(1)}, u32[]{:S(2)}, u32[]{:S(2)}) %collective-permute-start.2) | collective-permute-done | bytes 65568 | tf_op jit(solution)/shard_map/ppermute | solution.py:24
  11.0 0.0 collective-permute-done.below
  11.1 0.0 copy-start.2
  11.1 0.0 copy-start.4
  11.1 3.6 %collective-permute-start.1 = (bf16[9,32,256]{2,1,0:T(8,128)(2,1)S(1)}, bf16[9,32,256]{2,1,0:T(8,128)(2,1)S(1)}, u32[]{:S(2)}, u32[]{:S(2)}) collective-permute-start(bf16[9,32,256]{2,1,0:T(8,128)(2,1)S(1)} %fusion), channel_id=1, source_target_pairs={{0,1},{1,2},{2,3},{4,5},{5,6},{6,7},{8,9},{9,10},{10,11},{12,13},{... | collective-permute-start | bytes 442376 | tf_op jit(solution)/shard_map/ppermute | solution.py:24
  14.7 1.3 %collective-permute-start.3 = (bf16[3,64,128]{2,1,0:T(8,128)(2,1)S(1)}, bf16[3,64,128]{2,1,0:T(8,128)(2,1)S(1)}, u32[]{:S(2)}, u32[]{:S(2)}) collective-permute-start(bf16[3,64,128]{2,1,0:T(8,128)(2,1)S(1)} %pad_maximum_fusion.1), channel_id=1, source_target_pairs={{1,0},{2,1},{3,2},{5,4},{6,5},{7,6},{9,8},{10,9},{11,10},{13,12},{... | collective-permute-start | bytes 147464 | tf_op jit(solution)/shard_map/ppermute | solution.py:24
  16.0 0.0 copy-done.1
  16.1 3.3 %shard_map.59 = (bf16[1536,512]{1,0:T(8,128)(2,1)S(1)}, bf16[1536,512]{1,0:T(8,128)(2,1)S(1)}) custom-call(bf16[32,8,16,256]{3,2,1,0:T(8,128)(2,1)S(1)} %bitcast.30), custom_call_target="tpu_custom_call" | custom-call | flops 805306368 | bytes 8388608 | tf_op jit(solution)/shard_map/pallas_call | solution.py:252
  19.4 1.4 %collective-permute-done.3.cot_beside = bf16[3,64,128]{2,1,0:T(8,128)(2,1)S(1)} collective-permute-done((bf16[3,64,128]{2,1,0:T(8,128)(2,1)S(1)}, bf16[3,64,128]{2,1,0:T(8,128)(2,1)S(1)}, u32[]{:S(2)}, u32[]{:S(2)}) %collective-permute-start.3) | collective-permute-done | bytes 49184 | tf_op jit(solution)/shard_map/ppermute | solution.py:24
  20.7 0.0 collective-permute-done.1.beside
  20.7 0.0 copy-done.2
  20.7 0.0 copy-done.4
  20.7 5.9 %shard_map.61 = (f32[1120,128]{1,0:T(8,128)S(1)}, f32[1120,128]{1,0:T(8,128)S(1)}) custom-call(bf16[1536,512]{1,0:T(8,128)(2,1)S(1)} %get-tuple-element.22.even, bf16[1536,512]{1,0:T(8,128)(2,1)S(1)} %get-tuple-element.23.odd, bf16[512,256]{1,0:T(8,128)(2,1)S(1)} %collective-permute-done.below, bf16[9,32,256]{2,1,0:T(8,128)(2,1)S(1)} %collective-permute-done.1.beside, ...), custom_call_target="tpu_custom_call" | custom-call | tf_op jit(solution)/shard_map/pallas_call | solution.py:261
  26.7 1.6 %collective-permute-start.4 = (f32[1120,128]{1,0:T(8,128)S(1)}, f32[1120,128]{1,0:T(8,128)S(1)}, u32[]{:S(2)}, u32[]{:S(2)}) collective-permute-start(f32[1120,128]{1,0:T(8,128)S(1)} %get-tuple-element.27), channel_id=1, source_target_pairs={{0,4},{4,0},{1,5},{5,1},{2,6},{6,2},{3,7},{7,3},{8,12},{12,8},{9,1... | collective-permute-start | bytes 1720328 | tf_op jit(solution)/shard_map/ppermute | solution.py:280
  28.2 1.6 %collective-permute-done.4 = f32[1120,128]{1,0:T(8,128)S(1)} collective-permute-done((f32[1120,128]{1,0:T(8,128)S(1)}, f32[1120,128]{1,0:T(8,128)S(1)}, u32[]{:S(2)}, u32[]{:S(2)}) %collective-permute-start.4) | collective-permute-done | bytes 573472 | tf_op jit(solution)/shard_map/ppermute | solution.py:280
  29.8 0.1 add_convert_fusion
  29.9 10.2 %all_to_all.10 = bf16[4,280,128]{2,1,0:T(8,128)(2,1)S(1)} all-to-all(bf16[4,280,128]{2,1,0:T(8,128)(2,1)S(1)} %bitcast.38), channel_id=1, replica_groups=mesh['dp'=2,'gx'=2,'core'=2,'gy'=4] {'dp','gx'}, dimensions={0} | all-to-all | bytes 573440 | tf_op jit(solution)/shard_map/all_to_all | solution.py:282
  40.2 10.3 %all_to_all.11 = bf16[4,112,128]{2,1,0:T(8,128)(2,1)S(1)} all-to-all(bf16[4,112,128]{2,1,0:T(8,128)(2,1)S(1)} %pad_maximum_fusion), channel_id=1, replica_groups=mesh['dp'=2,'gx'=2,'core'=2,'gy'=4] {'gy'}, dimensions={0} | all-to-all | bytes 229376 | tf_op jit(solution)/shard_map/all_to_all | solution.py:286
  50.6 8.8 %all-gather = f32[896,128]{1,0:T(8,128)S(1)} all-gather(f32[112,128]{1,0:T(8,128)S(1)} %convert_reduce_fusion.1), channel_id=2, replica_groups=mesh['dp'=2,'gx'=2,'core'=2,'gy'=4] {'dp','gx','core'}, dimensions={0}, use_global_device_ids=true | all-gather | bytes 516096 | tf_op jit(solution)/shard_map/all_gather | solution.py:287
  59.5 1.0 %shard_map.62 = (f32[864,64]{1,0:T(8,128)}, f32[27,32,64]{2,1,0:T(8,128)}) custom-call(f32[8,112,128]{2,1,0:T(8,128)S(1)} %bitcast.31), custom_call_target="tpu_custom_call" | custom-call | tf_op jit(solution)/shard_map/pallas_call | solution.py:289
  (11 shorter events, 0.1 us)
Async XLA Ops:
  0.6 1.6 %copy-start = (bf16[1,32,8,16,256]{4,3,2,1,0:T(8,128)(2,1)S(1)}, bf16[1,32,8,16,256]{4,3,2,1,0:T(8,128)(2,1)}, u32[]{:S(2)}) copy-start(bf16[1,32,8,16,256]{4,3,2,1,0:T(8,128)(2,1)} %param.6) | copy-start | bytes 6291460
  2.2 4.9 %copy-start.3 = (bf16[1,128,2,4,64]{1,4,3,2,0:T(8,128)(2,1)S(1)}, bf16[1,128,2,4,64]{1,4,3,2,0:T(8,128)(2,1)}, u32[]{:S(2)}) copy-start(bf16[1,128,2,4,64]{1,4,3,2,0:T(8,128)(2,1)} %param.9) | copy-start | bytes 393220
  2.2 13.8 %copy-start.1 = (bf16[1,32,8,16,256]{4,3,2,1,0:T(8,128)(2,1)S(1)}, bf16[1,32,8,16,256]{4,3,2,1,0:T(8,128)(2,1)}, u32[]{:S(2)}) copy-start(bf16[1,32,8,16,256]{4,3,2,1,0:T(8,128)(2,1)} %param.6) | copy-start | bytes 6291460
  2.4 8.6 %collective-permute-start = (bf16[512,256]{1,0:T(8,128)(2,1)S(1)}, bf16[512,256]{1,0:T(8,128)(2,1)S(1)}, u32[]{:S(2)}, u32[]{:S(2)}) collective-permute-start(bf16[512,256]{1,0:T(8,128)(2,1)S(1)} %get-tuple-element.24), channel_id=1, source_target_pairs={{0,4},{4,8},{8,12},{1,5},{5,9},{9,13},{2,6},{6,10},{10,14},{3,7},{... | collective-permute-start | bytes 786440 | tf_op jit(solution)/shard_map/ppermute | solution.py:24
  5.8 5.2 %collective-permute-start.2 = (bf16[4,64,128]{2,1,0:T(8,128)(2,1)S(1)}, bf16[4,64,128]{2,1,0:T(8,128)(2,1)S(1)}, u32[]{:S(2)}, u32[]{:S(2)}) collective-permute-start(bf16[4,64,128]{2,1,0:T(8,128)(2,1)S(1)} %slice_bitcast_fusion), channel_id=1, source_target_pairs={{4,0},{8,4},{12,8},{5,1},{9,5},{13,9},{6,2},{10,6},{14,10},{7,3},{... | collective-permute-start | bytes 196616 | tf_op jit(solution)/shard_map/ppermute | solution.py:24
  11.1 9.7 %copy-start.2 = (bf16[128,64,3,3,3]{0,1,4,3,2:T(8,128)(2,1)S(1)}, bf16[128,64,3,3,3]{0,1,4,3,2:T(8,128)(2,1)}, u32[]{:S(2)}) copy-start(bf16[128,64,3,3,3]{0,1,4,3,2:T(8,128)(2,1)} %param.8) | copy-start | bytes 1327108
  11.1 9.7 %copy-start.4 = (bf16[64,32,3,3,3]{0,1,4,3,2:T(8,128)(2,1)S(1)}, bf16[64,32,3,3,3]{0,1,4,3,2:T(8,128)(2,1)}, u32[]{:S(2)}) copy-start(bf16[64,32,3,3,3]{0,1,4,3,2:T(8,128)(2,1)} %param.7) | copy-start | bytes 331780
  11.1 9.6 %collective-permute-start.1 = (bf16[9,32,256]{2,1,0:T(8,128)(2,1)S(1)}, bf16[9,32,256]{2,1,0:T(8,128)(2,1)S(1)}, u32[]{:S(2)}, u32[]{:S(2)}) collective-permute-start(bf16[9,32,256]{2,1,0:T(8,128)(2,1)S(1)} %fusion), channel_id=1, source_target_pairs={{0,1},{1,2},{2,3},{4,5},{5,6},{6,7},{8,9},{9,10},{10,11},{12,13},{... | collective-permute-start | bytes 442376 | tf_op jit(solution)/shard_map/ppermute | solution.py:24
  14.7 6.0 %collective-permute-start.3 = (bf16[3,64,128]{2,1,0:T(8,128)(2,1)S(1)}, bf16[3,64,128]{2,1,0:T(8,128)(2,1)S(1)}, u32[]{:S(2)}, u32[]{:S(2)}) collective-permute-start(bf16[3,64,128]{2,1,0:T(8,128)(2,1)S(1)} %pad_maximum_fusion.1), channel_id=1, source_target_pairs={{1,0},{2,1},{3,2},{5,4},{6,5},{7,6},{9,8},{10,9},{11,10},{13,12},{... | collective-permute-start | bytes 147464 | tf_op jit(solution)/shard_map/ppermute | solution.py:24
  26.7 3.2 %collective-permute-start.4 = (f32[1120,128]{1,0:T(8,128)S(1)}, f32[1120,128]{1,0:T(8,128)S(1)}, u32[]{:S(2)}, u32[]{:S(2)}) collective-permute-start(f32[1120,128]{1,0:T(8,128)S(1)} %get-tuple-element.27), channel_id=1, source_target_pairs={{0,4},{4,0},{1,5},{5,1},{2,6},{6,2},{3,7},{7,3},{8,12},{12,8},{9,1... | collective-permute-start | bytes 1720328 | tf_op jit(solution)/shard_map/ppermute | solution.py:280

commit v3 on v2

v3 whole, which is shorter than its diff:
```python
import functools
import math

import jax
import jax.numpy as jnp
from jax import lax
from jax.experimental import pallas as pl
from jax.experimental.pallas import tpu as pltpu
from jax.sharding import Mesh, PartitionSpec as P

BF16 = jnp.bfloat16
F32 = jnp.float32
NN = (((1,), (0,)), ((), ()))
NT = (((1,), (1,)), ((), ()))


def dot(a, b, dims=NN):
    return lax.dot_general(a, b, dims, preferred_element_type=F32)


def swapped(block, axis, first):
    count = lax.axis_size(axis)
    route = [(i, i + 1) for i in range(first, count - 1, 2)]
    return lax.ppermute(block, axis, route + [(j, i) for i, j in route])


def picking_matrix(breadth):
    half = breadth // 2
    row = lax.broadcasted_iota(jnp.int32, (breadth, 3 * half), 0)
    col = lax.broadcasted_iota(jnp.int32, (breadth, 3 * half), 1)
    offset = (col >= half).astype(jnp.int32) + (col >= 2 * half).astype(jnp.int32)
    lane = col - offset * half
    odd = (lane >= half // 2).astype(jnp.int32)
    cell = 2 * (lane - odd * (half // 2)) + odd
    return jnp.where(row == 2 * cell + offset - 1, 1.0, 0.0).astype(BF16)


def place(dst, row, lanes, piece):
    c1 = piece(0).shape[0]
    for a in range(3):
        dst[row + a * c1 : row + (a + 1) * c1, lanes] = piece(a).astype(BF16)


def spread_layer(rows, pick, tall, turned, height, put):
    c1 = rows.shape[0] // height
    rows = rows.astype(F32)
    for part in range(tall.shape[0]):
        tall[part] = rows[:, part * 128 : (part + 1) * 128]
    for y in range(height):
        parts = [tall[part, pl.ds(y, c1, stride=height), :] for part in range(tall.shape[0])]
        turned[y * c1 : (y + 1) * c1, :] = jnp.concatenate(parts, axis=1).astype(BF16)
    cells = dot(turned[...], pick)
    mx = cells.shape[1] // 3
    for y in range(height):
        put(y, lambda a: cells[y * c1 : (y + 1) * c1, a * mx : (a + 1) * mx])


def by_parity(axis, run, pair, cross):
    odd = lax.rem(lax.axis_index(axis), 2)
    pl.when(odd == 1)(lambda: run(pair, cross))
    pl.when(odd == 0)(lambda: run(cross, pair))


def first_kernel(rims, pair, cross):
    count = pair.shape[0]

    def fill(down, up):
        up[...] = rims[:count]
        down[: rims.shape[0] - count] = rims[count:]

    by_parity("core", fill, pair, cross)


def edge_kernel(dims, vol, cot, z_pair, z_cross, pair, cross, below, above, tall):
    c1, depth, height, breadth = dims
    dz, dy, dx, c3 = cot.shape

    def take(from_below, from_above):
        below[...] = from_below[...].astype(F32)[:, height - 8 :]
        above[...] = from_above[: dx // height, :, :c3].reshape(dx, c3)

    by_parity("core", take, z_pair, z_cross)

    def fill(down, up):
        for z in range(depth + 1):
            top = vol[:, z - 1].astype(F32)[:, height - 8 :] if z else below[...]
            top = top.reshape(c1 * 8, breadth)
            for part in range(breadth // 128):
                lanes = slice(part * 128, (part + 1) * 128)
                slot = (z * (breadth // 128) + part) % 4
                tall[slot] = top[:, lanes]
                up[z * c1 : (z + 1) * c1, lanes] = tall[slot, pl.ds(7, c1, stride=8), :].astype(BF16)
        for z in range(dz):
            down[z * dx : (z + 1) * dx, :c3] = cot[z, 0]
        down[dz * dx : (dz + 1) * dx, :c3] = above[...]

    by_parity("gy", fill, pair, cross)


def gather_kernel(dims, vol, even, odd, tall, turned):
    c1, depth, height, breadth = dims
    mx = breadth // 2
    pick = picking_matrix(breadth)
    for layer in range(depth):
        rows = vol[:, layer].reshape(c1 * height, breadth)
        dst = even if layer % 2 else odd
        lanes = slice(layer // 2 * mx, (layer // 2 + 1) * mx)
        put = lambda y, piece: place(dst, y * 3 * c1, lanes, piece)
        spread_layer(rows, pick, tall.at[layer % 2], turned.at[layer % 2], height, put)


def silu_and_slope(pre):
    sigma = jax.nn.sigmoid(pre)
    return (pre * sigma).astype(BF16), sigma * (1.0 + pre * (1.0 - sigma))


def put_active(act, active, y, c2, dy, mx):
    for z in range(active.shape[1] // mx):
        cls = (z % 2) * 2 + y % 2
        at = (z // 2) * dy + y // 2
        act[cls * c2 : (cls + 1) * c2, at * mx : (at + 1) * mx] = active[:, z * mx : (z + 1) * mx]


def put_pair(pairs, top, here, last):
    dx = here.shape[0]
    zero = jnp.zeros_like(here)
    moved = jnp.where(last, 0.0, pltpu.roll(here.astype(F32), dx - 1, 0)).astype(BF16)
    pairs[top : top + dx, :] = jnp.concatenate([zero, here, zero], axis=1)
    pairs[top + dx : top + 2 * dx, :] = jnp.concatenate([moved, zero, here], axis=1)


def classes_of(sz, sy):
    classes = [(pz, py) for pz in range(2) for py in range(2) if pz >= sz and py >= sy]
    return classes, [(0 if sz else 1 + pz, 0 if sy else 1 + py) for pz, py in classes]


def filters_of(kd, taps):
    return jnp.concatenate(
        [jnp.concatenate([kd[(az * 3 + ay) * 3 + ax] for ax in range(3)], axis=1) for az, ay in taps], axis=0
    )


def window(even, odd, side, y, az, blk, mx):
    rows = slice((2 * y - 1) * blk, (2 * y + 2) * blk)
    if az == 0:
        return jnp.concatenate([side[2 * y * blk : (2 * y + 3) * blk, :], even[rows, : even.shape[1] - mx]], axis=1)
    return odd[rows, :] if az == 1 else even[rows, :]


def early_kernel(dims, even, odd, z_pair, z_cross, cot, km, kd, rim_z, act, slope, pairs, back, deep, mid, below, above, tall, turned, grad):
    c1, c2, c3, depth, height, breadth = dims
    mz, my, mx = depth // 2, height // 2, breadth // 2
    dz, dy, dx = mz // 2, my // 2, mx // 2
    blk = 3 * c1

    def take(from_below, from_above):
        below[...] = from_below[...].reshape(c1 * height, breadth)
        above[...] = from_above[: dy * dx // height, :, :c3].reshape(dy, dx, c3)

    by_parity("core", take, z_pair, z_cross)
    put = lambda y, piece: place(rim_z, (y + 1) * blk, slice(0, mx), piece)
    spread_layer(below[...], picking_matrix(breadth), tall, turned, height, put)
    turned_km = km[...].astype(F32).T.astype(BF16)
    put_active(act, jnp.zeros((c2, mz * mx), BF16), 0, c2, dy, mx)
    for y in range(1, my):
        cells = jnp.concatenate([window(even, odd, rim_z, y, az, blk, mx) for az in range(3)], axis=0)
        active, slope[y] = silu_and_slope(dot(turned_km, cells))
        put_active(act, active, y, c2, dy, mx)

    last = lax.broadcasted_iota(jnp.int32, (dx, c3), 0) == dx - 1
    for z in range(dz + 1):
        for y in range(dy):
            put_pair(pairs, (z * (dy + 1) + y) * mx, above[y] if z == dz else cot[z, y], last)

    for sz in range(2):
        for sy in range(2):
            classes, taps = classes_of(sz, sy)
            lhs = jnp.concatenate([act[(pz * 2 + py) * c2 : (pz * 2 + py + 1) * c2, :] for pz, py in classes], axis=0)
            filters = filters_of(kd, taps)
            total = None
            for z in range(dz):
                start, count = z * dy * mx, (dy - sy) * mx
                top = ((z + sz) * (dy + 1) + sy) * mx
                cells = pairs[top : top + count, :]
                term = dot(lhs[:, start : start + count], cells)
                total = term if total is None else total + term
                grads = dot(filters, cells, NT)
                for n, (pz, py) in enumerate(classes):
                    rows = slice((pz * 2 + py) * c2, (pz * 2 + py + 1) * c2)
                    piece = grads[n * c2 : (n + 1) * c2]
                    if sz or sy:
                        piece = piece + back[rows, start : start + count]
                    back[rows, start : start + count] = piece
            for n, (az, ay) in enumerate(taps):
                deep[az * 3 + ay] = total[n * c2 : (n + 1) * c2]

    for y in range(1, my - 1):
        put_grad(grad.at[y - 1], back, slope[y], y, c2, dy, mx)
    for az in range(3):
        total = None
        for y in range(1, my - 1):
            term = dot(window(even, odd, rim_z, y, az, blk, mx), grad[y - 1], NT)
            total = term if total is None else total + term
        mid[az] = total


def put_grad(dst, back, slope, y, c2, dy, mx):
    for z in range(dst.shape[1] // mx):
        cls = (z % 2) * 2 + y % 2
        at = (z // 2) * dy + y // 2
        value = back[cls * c2 : (cls + 1) * c2, at * mx : (at + 1) * mx] * slope[:, z * mx : (z + 1) * mx]
        dst[:, z * mx : (z + 1) * mx] = value.astype(BF16)


def main_kernel(dims, even, odd, rim_z, act, slope, pairs, back_in, deep_in, mid_in, y_pair, y_cross, km, kd, keep, send, beside, cot_beside, corner, rim_even, rim_odd, rim_pairs, back, grad, sums):
    c1, c2, c3, depth, height, breadth, n_pl, n_gy = dims
    mz, my, mx = depth // 2, height // 2, breadth // 2
    dz, dy, dx = mz // 2, my // 2, mx // 2
    pick = picking_matrix(breadth)
    blk = 3 * c1

    def take(from_below, from_above):
        beside[...] = from_below[...]
        cot_beside[...] = from_above[: (dz + 1) * dx, :c3]

    by_parity("gy", take, y_pair, y_cross)

    for layer in range(depth + 1):
        rim = dot(beside[layer * c1 : (layer + 1) * c1, :], pick)
        if layer == 0:
            dst, at = corner, 0
        else:
            dst, at = (rim_odd, layer // 2) if layer % 2 else (rim_even, layer // 2 - 1)
        place(dst, 0, slice(at * mx, (at + 1) * mx), lambda a: rim[:, a * mx : (a + 1) * mx])
    upper = jnp.concatenate([rim_even[...], even[: 2 * blk, :]], axis=0)
    side = jnp.concatenate([corner[...], rim_z[blk : 3 * blk, :]], axis=0)
    first = [
        jnp.concatenate([side, upper[:, : (mz - 1) * mx]], axis=1),
        jnp.concatenate([rim_odd[...], odd[: 2 * blk, :]], axis=0),
        upper,
    ]

    turned_km = km[...].astype(F32).T.astype(BF16)
    active, low_slope = silu_and_slope(dot(turned_km, jnp.concatenate(first, axis=0)))

    last = lax.broadcasted_iota(jnp.int32, (dx, c3), 0) == dx - 1
    for z in range(dz + 1):
        put_pair(rim_pairs, z * mx, cot_beside[z * dx : (z + 1) * dx, :], last)

    back[...] = back_in[...]
    deep = {(az, ay): deep_in[az * 3 + ay] for az in range(3) for ay in range(3)}
    for sz in range(2):
        for sy in range(2):
            group = [(c, t) for c, t in zip(*classes_of(sz, sy)) if c[1] == sy]
            filters = filters_of(kd, [tap for _, tap in group])
            for z in range(dz):
                lanes = slice((z * dy + dy - 1) * mx, (z * dy + dy) * mx)
                rows = [slice((pz * 2 + py) * c2, (pz * 2 + py + 1) * c2) for (pz, py), _ in group]
                if sy:
                    cells = rim_pairs[(z + sz) * mx : (z + sz + 1) * mx, :]
                    lhs = [act[r, lanes] for r in rows]
                    grads = dot(filters, cells, NT)
                    for n, r in enumerate(rows):
                        back[r, lanes] = back[r, lanes] + grads[n * c2 : (n + 1) * c2]
                else:
                    top = (z + sz) * (dy + 1) * mx
                    cells = pairs[top : top + mx, :]
                    lhs = [active[:, (2 * z + pz) * mx : (2 * z + pz + 1) * mx] for (pz, py), _ in group]
                term = dot(jnp.concatenate(lhs, axis=0), cells)
                for n, (_, tap) in enumerate(group):
                    deep[tap] = deep[tap] + term[n * c2 : (n + 1) * c2]
    deep = {
        (az * 3 + ay) * 3 + ax: deep[az, ay][:, ax * c3 : (ax + 1) * c3]
        for az in range(3) for ay in range(3) for ax in range(3)
    }

    put_grad(grad.at[0], back, low_slope, 0, c2, dy, mx)
    put_grad(grad.at[1], back, slope[my - 1], my - 1, c2, dy, mx)
    mids = []
    for az in range(3):
        upper_row = dot(window(even, odd, rim_z, my - 1, az, blk, mx), grad[1], NT)
        mids.append(mid_in[az] + dot(first[az], grad[0], NT) + upper_row)
    mid = jnp.concatenate(mids, axis=0)

    share = c3 // n_gy
    per = 448 // (2 * n_pl)
    chunk = (n_gy + 1) * per

    def spread(value, first, offset):
        done = 0
        while done < value.shape[0]:
            k, r = divmod(first + done, per)
            count = min(per - r, value.shape[0] - done)
            core, start = k % 2, k // 2 * chunk + offset + r
            sums[core, start : start + count, :] = value[done : done + count]
            done += count

    for slab in range(14):
        second = deep[2 * slab + 1] if 2 * slab + 1 < 27 else jnp.zeros((c2, c3), F32)
        turned = jnp.concatenate([deep[2 * slab], second], axis=0).T
        for g in range(n_gy):
            spread(turned[g * share : (g + 1) * share], slab * share, g * per)
    half = mid.shape[0] // 2
    packed = jnp.concatenate([mid[:half], mid[half:]], axis=1)
    packed = jnp.concatenate([packed, jnp.zeros((448 - half, 128), F32)], axis=0)
    spread(packed, 0, n_gy * per)
    core = lax.axis_index("core")
    keep[...] = sums[core]
    send[...] = sums[1 - core]


def last_kernel(dims, scales, got, mid_out, deep_out):
    n_all, share, c2, per = dims
    whole = got[...]
    deep = whole[:, :per].reshape(n_all * per, 128) * scales[1]
    mid = whole[:, per:].reshape(n_all * per, 128) * scales[0]
    for a in range(27):
        deep_out[a] = deep[(a // 2) * share : (a // 2 + 1) * share, (a % 2) * c2 : (a % 2 + 1) * c2]
    mid_out[:432] = mid[:432, :64]
    mid_out[432:] = mid[:432, 64:]


def on_device(volume, kernel_mid, kernel_deep, cotangent):
    n_dp = lax.axis_size("dp")
    gz = ("gx", "core")
    n_gz = lax.axis_size(gz)
    n_gy = lax.axis_size("gy")
    samples, c1, depth, height, breadth = volume.shape
    c2, c3 = kernel_mid.shape[0], kernel_deep.shape[0]
    count_mid = n_dp * samples * (n_gz * depth // 2) * (n_gy * height // 2) * (breadth // 2)
    count_deep = n_dp * samples * (n_gz * depth // 4) * (n_gy * height // 4) * (breadth // 4)
    mz, my, mx = depth // 2, height // 2, breadth // 2
    dz, dy, dx = mz // 2, my // 2, mx // 2
    n_pl = n_dp * n_gz // 2
    vol = volume[0]
    cot = cotangent[0].transpose(1, 2, 3, 0)
    in_vmem = pl.BlockSpec(memory_space=pltpu.VMEM)
    cot_layer = jnp.pad(cot[0].reshape(-1, height, c3), ((0, 0), (0, 0), (0, breadth - c3)))
    rims = jnp.concatenate([vol[:, -1], cot_layer], axis=0)
    payload = jax.ShapeDtypeStruct((c1, height, breadth), BF16)
    pair, cross = pl.pallas_call(
        first_kernel,
        out_shape=(payload, payload),
        in_specs=[in_vmem],
        out_specs=(in_vmem, in_vmem),
        compiler_params=pltpu.CompilerParams(vmem_limit_bytes=4 * 1024 * 1024),
    )(rims)
    z_cross = swapped(cross, gz, 1)
    z_pair = swapped(pair, gz, 0)
    blk = 3 * c1
    own_cells = jax.ShapeDtypeStruct((height * blk, mz * mx), BF16)
    even, odd = pl.pallas_call(
        functools.partial(gather_kernel, (c1, depth, height, breadth)),
        out_shape=(own_cells, own_cells),
        in_specs=[in_vmem],
        out_specs=(in_vmem, in_vmem),
        scratch_shapes=[
            pltpu.VMEM((2, breadth // 128, c1 * height, 128), F32),
            pltpu.VMEM((2, c1 * height, breadth), BF16),
        ],
        cost_estimate=pl.CostEstimate(flops=2 * c1 * depth * height * breadth * 3 * mx, bytes_accessed=8 << 20, transcendentals=0),
        compiler_params=pltpu.CompilerParams(vmem_limit_bytes=24 * 1024 * 1024),
    )(vol)
    payload = jax.ShapeDtypeStruct(((depth + 1) * c1, breadth), BF16)
    pair, cross = pl.pallas_call(
        functools.partial(edge_kernel, (c1, depth, height, breadth)),
        out_shape=(payload, payload),
        in_specs=[in_vmem] * 4,
        out_specs=(in_vmem, in_vmem),
        scratch_shapes=[
            pltpu.VMEM((c1, 8, breadth), F32),
            pltpu.VMEM((dx, c3), BF16),
            pltpu.VMEM((4, c1 * 8, 128), F32),
        ],
        compiler_params=pltpu.CompilerParams(vmem_limit_bytes=16 * 1024 * 1024),
    )(vol, cot, z_pair, z_cross)
    pair, cross, even, odd = lax.optimization_barrier((pair, cross, even, odd))
    y_pair, y_cross = swapped(pair, "gy", 0), swapped(cross, "gy", 1)
    km = kernel_mid.transpose(2, 3, 4, 1, 0).reshape(27 * c1, c2)
    kd = kernel_deep.transpose(2, 3, 4, 1, 0).reshape(27, c2, c3)

    share = c3 // n_gy
    per = 448 // (2 * n_pl)
    chunk = (n_gy + 1) * per
    rim_z, act, slope, pairs, back, deep, mid = pl.pallas_call(
        functools.partial(early_kernel, (c1, c2, c3, depth, height, breadth)),
        out_shape=(
            jax.ShapeDtypeStruct(((height + 1) * blk, mx), BF16),
            jax.ShapeDtypeStruct((4 * c2, dz * dy * mx), BF16),
            jax.ShapeDtypeStruct((my, c2, mz * mx), F32),
            jax.ShapeDtypeStruct(((dz + 1) * (dy + 1) * mx, 3 * c3), BF16),
            jax.ShapeDtypeStruct((4 * c2, dz * dy * mx), F32),
            jax.ShapeDtypeStruct((9, c2, 3 * c3), F32),
            jax.ShapeDtypeStruct((3, 3 * blk, c2), F32),
        ),
        in_specs=[in_vmem] * 7,
        out_specs=(in_vmem,) * 7,
        scratch_shapes=[
            pltpu.VMEM((c1 * height, breadth), BF16),
            pltpu.VMEM((dy, dx, c3), BF16),
            pltpu.VMEM((breadth // 128, c1 * height, 128), F32),
            pltpu.VMEM((c1 * height, breadth), BF16),
            pltpu.VMEM((my - 2, c2, mz * mx), BF16),
        ],
        cost_estimate=pl.CostEstimate(flops=2 * c1 * depth * height * breadth * 3 * mx, bytes_accessed=8 << 20, transcendentals=0),
        compiler_params=pltpu.CompilerParams(vmem_limit_bytes=24 * 1024 * 1024),
    )(even, odd, z_pair, z_cross, cot, km, kd)
    keep, send = pl.pallas_call(
        functools.partial(main_kernel, (c1, c2, c3, depth, height, breadth, n_pl, n_gy)),
        out_shape=(jax.ShapeDtypeStruct((n_pl * chunk, 128), F32), jax.ShapeDtypeStruct((n_pl * chunk, 128), F32)),
        in_specs=[in_vmem] * 13,
        out_specs=(in_vmem, in_vmem),
        scratch_shapes=[
            pltpu.VMEM(((depth + 1) * c1, breadth), BF16),
            pltpu.VMEM(((dz + 1) * dx, c3), BF16),
            pltpu.VMEM((blk, mx), BF16),
            pltpu.VMEM((blk, mz * mx), BF16),
            pltpu.VMEM((blk, mz * mx), BF16),
            pltpu.VMEM(((dz + 1) * mx, 3 * c3), BF16),
            pltpu.VMEM((4 * c2, dz * dy * mx), F32),
            pltpu.VMEM((2, c2, mz * mx), BF16),
            pltpu.VMEM((2, n_pl * chunk, 128), F32),
        ],
        compiler_params=pltpu.CompilerParams(vmem_limit_bytes=32 * 1024 * 1024),
    )(even, odd, rim_z, act, slope, pairs, back, deep, mid, y_pair, y_cross, km, kd)
    other = lax.ppermute(send, "core", [(0, 1), (1, 0)])
    pair = (keep + other).astype(BF16).reshape(n_pl, chunk, 128)
    own = jnp.sum(lax.all_to_all(pair, ("dp", "gx"), 0, 0).astype(F32), axis=0)
    deep_own = own[: n_gy * per].reshape(n_gy, per, 128)
    mid_own = jnp.broadcast_to(own[n_gy * per :], (n_gy, per, 128))
    column = jnp.concatenate([deep_own, mid_own], axis=1).astype(BF16)
    own = jnp.sum(lax.all_to_all(column, "gy", 0, 0).astype(F32), axis=0)
    whole = lax.all_gather(own, ("dp", "gx", "core"), axis=0)
    scales = (1.0 / math.sqrt(count_mid), 1.0 / math.sqrt(count_deep))
    mid, deep = pl.pallas_call(
        functools.partial(last_kernel, (2 * n_pl, share, c2, per), scales),
        out_shape=(jax.ShapeDtypeStruct((27 * c1, c2), F32), jax.ShapeDtypeStruct((27, share, c2), F32)),
        in_specs=[in_vmem],
        out_specs=(in_vmem, in_vmem),
        compiler_params=pltpu.CompilerParams(vmem_limit_bytes=24 * 1024 * 1024),
    )(whole)
    mid = mid.reshape(3, 3, 3, c1, c2).transpose(4, 3, 0, 1, 2)
    deep = deep.reshape(3, 3, 3, share, c2).transpose(3, 4, 0, 1, 2)
    return mid, deep


def solution(mesh):
    n_dp, n_gz, n_gy = (mesh.shape[name] for name in ("dp", "gz", "gy"))
    split = Mesh(mesh.devices.reshape(n_dp, n_gz // 2, 2, n_gy), ("dp", "gx", "core", "gy"))
    by_cells = P("dp", None, ("gx", "core"), "gy", None)
    in_specs = (by_cells, P(), P(), by_cells)
    out_specs = (P(), P("gy", None, None, None, None))
    return jax.shard_map(
        on_device, mesh=split, in_specs=in_specs, out_specs=out_specs, check_vma=False
    )
```

time: 60.9 us -> 55.2 us (0.906)
  waiting for transfers between devices: 6.89 us -> 1.62 us
  starting transfers between devices: 10.3 us -> 8.31 us
  local copies, waits for them, and re-layouts: 2.52 us -> 3.44 us
  blocking collectives: 29.4 us -> 30.1 us
    ppermute x4, waiting for transfers between devices: 5.28 us -> 0.01 us  [swapped(): return lax.ppermute(block, axis, route + [(j, i) for i, j in route])]
    pallas_call x0 -> x2, Pallas kernels: none -> 5.12 us  [the longest x1 5.08 us: on_device(): pl.pallas_call(functools.partial(early_kernel, (c1, c2, c3, depth, height...]
    ppermute x4, starting transfers between devices: 8.7 us -> 4.5 us  [swapped(): return lax.ppermute(block, axis, route + [(j, i) for i, j in route])]
    pallas_call x1, Pallas kernels: 5.92 us -> 1.82 us  [on_device(): pl.pallas_call(functools.partial(main_kernel, (c1, c2, c3, depth, height,...]
    ppermute x1, starting transfers between devices: 1.57 us -> 3.81 us  [on_device(): other = lax.ppermute(send, 'core', [(0, 1), (1, 0)])]
    pallas_call x1, Pallas kernels: 3.3 us -> 2.09 us  [on_device(): pl.pallas_call(functools.partial(gather_kernel, (c1, depth, height, bread...]
    all_to_all x1, blocking collectives: 10.3 us -> 11.3 us  [on_device(): own = jnp.sum(lax.all_to_all(column, 'gy', 0, 0).astype(F32), axis=0)]
    slice x2 -> x1, local copies, waits for them, and re-layouts: 0.04 us -> 0.85 us  [on_device(): cot[0].reshape(-1, height, c3)]
  transfers between devices with their start and end apart: 5 -> 5, of which waited for: 3 -> 1; matrix products, arithmetic and copies ran while one was open for 1% -> 0% of each run, Pallas kernels for 5% -> 13%
where the time goes in v3:
time: 55.2 us; the launch traced here: 54.8 us
  blocking collectives  30.1 us (55%)
  Pallas kernels  10.3 us (19%)
  starting transfers between devices  8.31 us (15%)
  local copies, waits for them, and re-layouts  3.44 us (6%)
  waiting for transfers between devices  1.62 us (3%)
  between operations  0.81 us (1%)
    all_to_all x1, blocking collectives, on_device(): own = jnp.sum(lax.all_to_all(column, 'gy', 0, 0).astype(F32), axis=0)  11.3 us
    all_to_all x1, blocking collectives, on_device(): own = jnp.sum(lax.all_to_all(pair, ('dp', 'gx'), 0, 0).astype(F32), axis=0)  9.95 us
    all_gather x1, blocking collectives, on_device(): whole = lax.all_gather(own, ('dp', 'gx', 'core'), axis=0)  8.84 us
    pallas_call x1, Pallas kernels, on_device(): pl.pallas_call(functools.partial(early_kernel, (c1, c2, c3, depth, height...  5.08 us
    ppermute x4, starting transfers between devices, swapped(): return lax.ppermute(block, axis, route + [(j, i) for i, j in route])  4.5 us
    ppermute x1, starting transfers between devices, on_device(): other = lax.ppermute(send, 'core', [(0, 1), (1, 0)])  3.81 us
    pallas_call x1, Pallas kernels, on_device(): pl.pallas_call(functools.partial(gather_kernel, (c1, depth, height, bread...  2.09 us
    pallas_call x1, Pallas kernels, on_device(): pl.pallas_call(functools.partial(main_kernel, (c1, c2, c3, depth, height,...  1.82 us
  transfers between devices with their start and end apart: 5, of which 1 were waited for; matrix products, arithmetic and copies ran while one was open for 0% of the time, Pallas kernels for 13%

profile of v3, /device:TPU:0, one launch (start us, length us, event | category | flops | bytes accessed | tf_op | source)
XLA Modules:
  0.0 54.8 jit_solution(2517882452622820085)
XLA Ops:
  0.6 0.8 %slice.18 = bf16[1,4,64,128]{3,2,1,0:T(8,128)(2,1)S(1)} slice(bf16[2,4,64,128]{3,2,1,0:T(8,128)(2,1)} %bitcast.30), slice={[0:1], [0:4], [0:64], [0:128]} | slice | bytes 131072 | tf_op jit(solution)/shard_map/slice | solution.py:338
  1.5 1.0 %slice_bitcast_fusion = bf16[32,16,256]{2,1,0:T(8,128)(2,1)S(1)} fusion(bf16[32,8,16,256]{3,2,1,0:T(8,128)(2,1)} %bitcast.22), kind=kLoop, calls=%fused_computation.5 | loop fusion | bytes 524288 | tf_op jit(solution)/shard_map/squeeze | solution.py:339
  2.5 0.0 copy-start.3
  2.6 0.5 collective-permute-start
  3.1 0.7 %collective-permute-start.1 = (bf16[32,16,256]{2,1,0:T(8,128)(2,1)S(1)}, bf16[32,16,256]{2,1,0:T(8,128)(2,1)S(1)}, u32[]{:S(2)}, u32[]{:S(2)}) collective-permute-start(bf16[32,16,256]{2,1,0:T(8,128)(2,1)S(1)} %get-tuple-element.24), channel_id=1, source_target_pairs={{4,8},{8,4},{5,9},{9,5},{6,10},{10,6},{7,11},{11,7},{20,24},{24,20... | collective-permute-start | bytes 786440 | tf_op jit(solution)/shard_map/ppermute | solution.py:24
  3.7 0.0 copy-start
  3.8 1.6 %copy-done = bf16[1,32,8,16,256]{4,3,2,1,0:T(8,128)(2,1)S(1)} copy-done((bf16[1,32,8,16,256]{4,3,2,1,0:T(8,128)(2,1)S(1)}, bf16[1,32,8,16,256]{4,3,2,1,0:T(8,128)(2,1)}, u32[]{:S(2)}) %copy-start) | copy-done | bytes 2097176
  5.3 2.1 %shard_map.61 = (bf16[1536,512]{1,0:T(8,128)(2,1)S(1)}, bf16[1536,512]{1,0:T(8,128)(2,1)S(1)}) custom-call(bf16[32,8,16,256]{3,2,1,0:T(8,128)(2,1)S(1)} %bitcast.23), custom_call_target="tpu_custom_call" | custom-call | flops 805306368 | bytes 8388608 | tf_op jit(solution)/shard_map/pallas_call | solution.py:352
  7.4 0.0 copy-start.1
  7.4 0.0 copy-start.2
  7.5 0.0 collective-permute-done.z_pair
  7.5 0.0 collective-permute-done.1.z_cross
  7.5 0.0 copy-done.3
  7.5 0.2 shard_map.60
  7.7 2.7 %collective-permute-start.2 = (bf16[288,256]{1,0:T(8,128)(2,1)S(1)}, bf16[288,256]{1,0:T(8,128)(2,1)S(1)}, u32[]{:S(2)}, u32[]{:S(2)}) collective-permute-start(bf16[288,256]{1,0:T(8,128)(2,1)S(1)} %get-tuple-element.38), channel_id=1, source_target_pairs={{0,1},{2,3},{1,0},{3,2},{4,5},{6,7},{5,4},{7,6},{8,9},{10,11},{9,8... | collective-permute-start | bytes 442376 | tf_op jit(solution)/shard_map/ppermute | solution.py:24
  10.4 0.7 %collective-permute-start.3 = (bf16[288,256]{1,0:T(8,128)(2,1)S(1)}, bf16[288,256]{1,0:T(8,128)(2,1)S(1)}, u32[]{:S(2)}, u32[]{:S(2)}) collective-permute-start(bf16[288,256]{1,0:T(8,128)(2,1)S(1)} %get-tuple-element.39), channel_id=1, source_target_pairs={{1,2},{2,1},{5,6},{6,5},{9,10},{10,9},{13,14},{14,13},{17,18},{18,... | collective-permute-start | bytes 442376 | tf_op jit(solution)/shard_map/ppermute | solution.py:24
  11.1 0.0 copy-done.1
  11.1 0.0 copy-done.2
  11.1 5.1 %shard_map.62 = (bf16[1632,128]{1,0:T(8,128)(2,1)S(1)}, bf16[256,1024]{1,0:T(8,128)(2,1)S(1)}, f32[8,64,512]{2,1,0:T(8,128)S(1)}, bf16[1920,384]{1,0:T(8,128)(2,...) custom-call(bf16[1536,512]{1,0:T(8,128)(2,1)S(1)} %get-tuple-element.29.even, ...), custom_call_target="tpu_custom_call" | custom-call | flops 805306368 | bytes 8388608 | tf_op jit(solution)/shard_map/pallas_call | solution.py:385
  16.2 0.0 collective-permute-done.2.y_pair
  16.2 0.0 collective-permute-done.3.y_cross
  16.2 1.8 %shard_map.63 = (f32[1120,128]{1,0:T(8,128)S(1)}, f32[1120,128]{1,0:T(8,128)S(1)}) custom-call(bf16[1536,512]{1,0:T(8,128)(2,1)S(1)} %get-tuple-element.29.even, bf16[1536,512]{1,0:T(8,128)(2,1)S(1)} %get-tuple-element.30.odd, bf16[1632,128]{1,0:T(8,128)(2,1)S(1)} %get-tuple-element.31.rim_z, bf16[256,1024]{1,0:T(8,128)(2,1)S(1)} %get-tuple-element.32.act, ...), custom_call_target="tpu_custom_call" | custom-call | tf_op jit(solution)/shard_map/pallas_call | solution.py:408
  18.0 3.8 %collective-permute-start.4 = (f32[1120,128]{1,0:T(8,128)S(1)}, f32[1120,128]{1,0:T(8,128)S(1)}, u32[]{:S(2)}, u32[]{:S(2)}) collective-permute-start(f32[1120,128]{1,0:T(8,128)S(1)} %get-tuple-element.41), channel_id=1, source_target_pairs={{0,4},{4,0},{1,5},{5,1},{2,6},{6,2},{3,7},{7,3},{8,12},{12,8},{9,1... | collective-permute-start | bytes 1720328 | tf_op jit(solution)/shard_map/ppermute | solution.py:426
  21.8 1.6 %collective-permute-done.4 = f32[1120,128]{1,0:T(8,128)S(1)} collective-permute-done((f32[1120,128]{1,0:T(8,128)S(1)}, f32[1120,128]{1,0:T(8,128)S(1)}, u32[]{:S(2)}, u32[]{:S(2)}) %collective-permute-start.4) | collective-permute-done | bytes 573472 | tf_op jit(solution)/shard_map/ppermute | solution.py:426
  23.4 0.1 add_convert_fusion
  23.5 9.9 %all_to_all.10 = bf16[4,280,128]{2,1,0:T(8,128)(2,1)S(1)} all-to-all(bf16[4,280,128]{2,1,0:T(8,128)(2,1)S(1)} %bitcast.33), channel_id=1, replica_groups=mesh['dp'=2,'gx'=2,'core'=2,'gy'=4] {'dp','gx'}, dimensions={0} | all-to-all | bytes 573440 | tf_op jit(solution)/shard_map/all_to_all | solution.py:428
  33.6 11.3 %all_to_all.11 = bf16[4,112,128]{2,1,0:T(8,128)(2,1)S(1)} all-to-all(bf16[4,112,128]{2,1,0:T(8,128)(2,1)S(1)} %pad_maximum_fusion), channel_id=1, replica_groups=mesh['dp'=2,'gx'=2,'core'=2,'gy'=4] {'gy'}, dimensions={0} | all-to-all | bytes 229376 | tf_op jit(solution)/shard_map/all_to_all | solution.py:432
  44.9 8.8 %all-gather = f32[896,128]{1,0:T(8,128)S(1)} all-gather(f32[112,128]{1,0:T(8,128)S(1)} %convert_reduce_fusion.1), channel_id=2, replica_groups=mesh['dp'=2,'gx'=2,'core'=2,'gy'=4] {'dp','gx','core'}, dimensions={0}, use_global_device_ids=true | all-gather | bytes 516096 | tf_op jit(solution)/shard_map/all_gather | solution.py:433
  53.8 1.0 %shard_map.64 = (f32[864,64]{1,0:T(8,128)}, f32[27,32,64]{2,1,0:T(8,128)}) custom-call(f32[8,112,128]{2,1,0:T(8,128)S(1)} %bitcast.25), custom_call_target="tpu_custom_call" | custom-call | tf_op jit(solution)/shard_map/pallas_call | solution.py:435
  (8 shorter events, 0.2 us)
Async XLA Ops:
  2.5 5.0 %copy-start.3 = (bf16[1,128,2,4,64]{1,4,3,2,0:T(8,128)(2,1)S(1)}, bf16[1,128,2,4,64]{1,4,3,2,0:T(8,128)(2,1)}, u32[]{:S(2)}) copy-start(bf16[1,128,2,4,64]{1,4,3,2,0:T(8,128)(2,1)} %param.7) | copy-start | bytes 393220
  2.6 4.9 %collective-permute-start = (bf16[32,16,256]{2,1,0:T(8,128)(2,1)S(1)}, bf16[32,16,256]{2,1,0:T(8,128)(2,1)S(1)}, u32[]{:S(2)}, u32[]{:S(2)}) collective-permute-start(bf16[32,16,256]{2,1,0:T(8,128)(2,1)S(1)} %get-tuple-element.23), channel_id=1, source_target_pairs={{0,4},{8,12},{4,0},{12,8},{1,5},{9,13},{5,1},{13,9},{2,6},{10,14},... | collective-permute-start | bytes 786440 | tf_op jit(solution)/shard_map/ppermute | solution.py:24
  3.1 4.4 %collective-permute-start.1 = (bf16[32,16,256]{2,1,0:T(8,128)(2,1)S(1)}, bf16[32,16,256]{2,1,0:T(8,128)(2,1)S(1)}, u32[]{:S(2)}, u32[]{:S(2)}) collective-permute-start(bf16[32,16,256]{2,1,0:T(8,128)(2,1)S(1)} %get-tuple-element.24), channel_id=1, source_target_pairs={{4,8},{8,4},{5,9},{9,5},{6,10},{10,6},{7,11},{11,7},{20,24},{24,20... | collective-permute-start | bytes 786440 | tf_op jit(solution)/shard_map/ppermute | solution.py:24
  3.7 1.6 %copy-start = (bf16[1,32,8,16,256]{4,3,2,1,0:T(8,128)(2,1)S(1)}, bf16[1,32,8,16,256]{4,3,2,1,0:T(8,128)(2,1)}, u32[]{:S(2)}) copy-start(bf16[1,32,8,16,256]{4,3,2,1,0:T(8,128)(2,1)} %param.4) | copy-start | bytes 6291460
  7.4 3.6 %copy-start.1 = (bf16[128,64,3,3,3]{0,1,4,3,2:T(8,128)(2,1)S(1)}, bf16[128,64,3,3,3]{0,1,4,3,2:T(8,128)(2,1)}, u32[]{:S(2)}) copy-start(bf16[128,64,3,3,3]{0,1,4,3,2:T(8,128)(2,1)} %param.6) | copy-start | bytes 1327108
  7.4 3.6 %copy-start.2 = (bf16[64,32,3,3,3]{0,1,4,3,2:T(8,128)(2,1)S(1)}, bf16[64,32,3,3,3]{0,1,4,3,2:T(8,128)(2,1)}, u32[]{:S(2)}) copy-start(bf16[64,32,3,3,3]{0,1,4,3,2:T(8,128)(2,1)} %param.5) | copy-start | bytes 331780
  7.7 8.4 %collective-permute-start.2 = (bf16[288,256]{1,0:T(8,128)(2,1)S(1)}, bf16[288,256]{1,0:T(8,128)(2,1)S(1)}, u32[]{:S(2)}, u32[]{:S(2)}) collective-permute-start(bf16[288,256]{1,0:T(8,128)(2,1)S(1)} %get-tuple-element.38), channel_id=1, source_target_pairs={{0,1},{2,3},{1,0},{3,2},{4,5},{6,7},{5,4},{7,6},{8,9},{10,11},{9,8... | collective-permute-start | bytes 442376 | tf_op jit(solution)/shard_map/ppermute | solution.py:24
  10.4 5.8 %collective-permute-start.3 = (bf16[288,256]{1,0:T(8,128)(2,1)S(1)}, bf16[288,256]{1,0:T(8,128)(2,1)S(1)}, u32[]{:S(2)}, u32[]{:S(2)}) collective-permute-start(bf16[288,256]{1,0:T(8,128)(2,1)S(1)} %get-tuple-element.39), channel_id=1, source_target_pairs={{1,2},{2,1},{5,6},{6,5},{9,10},{10,9},{13,14},{14,13},{17,18},{18,... | collective-permute-start | bytes 442376 | tf_op jit(solution)/shard_map/ppermute | solution.py:24
  18.0 5.4 %collective-permute-start.4 = (f32[1120,128]{1,0:T(8,128)S(1)}, f32[1120,128]{1,0:T(8,128)S(1)}, u32[]{:S(2)}, u32[]{:S(2)}) collective-permute-start(f32[1120,128]{1,0:T(8,128)S(1)} %get-tuple-element.41), channel_id=1, source_target_pairs={{0,4},{4,0},{1,5},{5,1},{2,6},{6,2},{3,7},{7,3},{8,12},{12,8},{9,1... | collective-permute-start | bytes 1720328 | tf_op jit(solution)/shard_map/ppermute | solution.py:426

commit v4 on v3

--- a/solution.py
+++ b/solution.py
@@ -59,16 +59,6 @@
     odd = lax.rem(lax.axis_index(axis), 2)
     pl.when(odd == 1)(lambda: run(pair, cross))
     pl.when(odd == 0)(lambda: run(cross, pair))
-
-
-def first_kernel(rims, pair, cross):
-    count = pair.shape[0]
-
-    def fill(down, up):
-        up[...] = rims[:count]
-        down[: rims.shape[0] - count] = rims[count:]
-
-    by_parity("core", fill, pair, cross)
 
 
 def edge_kernel(dims, vol, cot, z_pair, z_cross, pair, cross, below, above, tall):
@@ -212,7 +202,7 @@
         dst[:, z * mx : (z + 1) * mx] = value.astype(BF16)
 
 
-def main_kernel(dims, even, odd, rim_z, act, slope, pairs, back_in, deep_in, mid_in, y_pair, y_cross, km, kd, keep, send, beside, cot_beside, corner, rim_even, rim_odd, rim_pairs, back, grad, sums):
+def main_kernel(dims, even, odd, rim_z, act, slope, pairs, back_in, deep_in, mid_in, y_cross, y_pair, km, kd, keep, send, beside, cot_beside, corner, rim_even, rim_odd, rim_pairs, back, grad, sums):
     c1, c2, c3, depth, height, breadth, n_pl, n_gy = dims
     mz, my, mx = depth // 2, height // 2, breadth // 2
     dz, dy, dx = mz // 2, my // 2, mx // 2
@@ -335,16 +325,11 @@
     vol = volume[0]
     cot = cotangent[0].transpose(1, 2, 3, 0)
     in_vmem = pl.BlockSpec(memory_space=pltpu.VMEM)
-    cot_layer = jnp.pad(cot[0].reshape(-1, height, c3), ((0, 0), (0, 0), (0, breadth - c3)))
-    rims = jnp.concatenate([vol[:, -1], cot_layer], axis=0)
-    payload = jax.ShapeDtypeStruct((c1, height, breadth), BF16)
-    pair, cross = pl.pallas_call(
-        first_kernel,
-        out_shape=(payload, payload),
-        in_specs=[in_vmem],
-        out_specs=(in_vmem, in_vmem),
-        compiler_params=pltpu.CompilerParams(vmem_limit_bytes=4 * 1024 * 1024),
-    )(rims)
+    layer = vol.reshape(c1, depth * height, breadth)[:, -height:]
+    flat = cot.reshape(-1, height, c3)
+    cot_layer = jnp.pad(flat, ((0, c1 - flat.shape[0]), (0, 0), (0, breadth - c3)))
+    odd = lax.axis_index("core") == 1
+    cross, pair = jnp.where(odd, layer, cot_layer), jnp.where(odd, cot_layer, layer)
     z_cross = swapped(cross, gz, 1)
     z_pair = swapped(pair, gz, 0)
     blk = 3 * c1
@@ -422,7 +407,7 @@
             pltpu.VMEM((2, n_pl * chunk, 128), F32),
         ],
         compiler_params=pltpu.CompilerParams(vmem_limit_bytes=32 * 1024 * 1024),
-    )(even, odd, rim_z, act, slope, pairs, back, deep, mid, y_pair, y_cross, km, kd)
+    )(even, odd, rim_z, act, slope, pairs, back, deep, mid, y_cross, y_pair, km, kd)
     other = lax.ppermute(send, "core", [(0, 1), (1, 0)])
     pair = (keep + other).astype(BF16).reshape(n_pl, chunk, 128)
     own = jnp.sum(lax.all_to_all(pair, ("dp", "gx"), 0, 0).astype(F32), axis=0)

time: 55.2 us -> 54 us (0.978)
  blocking collectives: 30.1 us -> 27.6 us
  starting transfers between devices: 8.31 us -> 10.2 us
  local copies, waits for them, and re-layouts: 3.44 us -> 1.63 us
  other arithmetic: 0.18 us -> 1.29 us
    ppermute x4, starting transfers between devices: 4.5 us -> 10.2 us  [swapped(): return lax.ppermute(block, axis, route + [(j, i) for i, j in route])]
    ppermute x1, starting transfers between devices: 3.81 us -> 0.07 us  [on_device(): other = lax.ppermute(send, 'core', [(0, 1), (1, 0)])]
    all_to_all x1, blocking collectives: 11.3 us -> 8.29 us  [on_device(): own = jnp.sum(lax.all_to_all(column, 'gy', 0, 0).astype(F32), axis=0)]
    select_n x0 -> x1, other arithmetic: none -> 1.14 us  [on_device(): jnp.where(odd, layer, cot_layer)]
    squeeze x1 -> x0, local copies, waits for them, and re-layouts: 0.97 us -> none  [on_device(): rims = jnp.concatenate([vol[:, -1], cot_layer], axis=0)]
    slice x1 -> x0, local copies, waits for them, and re-layouts: 0.85 us -> none  [on_device(): cot[0].reshape(-1, height, c3)]
where the time goes in v4:
time: 54 us; the launch traced here: 53.7 us
  blocking collectives  27.6 us (51%)
  Pallas kernels  10.3 us (19%)
  starting transfers between devices  10.2 us (19%)
  waiting for transfers between devices  1.98 us (4%)
  local copies, waits for them, and re-layouts  1.63 us (3%)
  other arithmetic  1.29 us (2%)
  between operations  0.79 us (1%)
    all_to_all x1, blocking collectives, on_device(): own = jnp.sum(lax.all_to_all(pair, ('dp', 'gx'), 0, 0).astype(F32), axis=0)  10.4 us
    ppermute x4, starting transfers between devices, swapped(): return lax.ppermute(block, axis, route + [(j, i) for i, j in route])  10.2 us
    all_gather x1, blocking collectives, on_device(): whole = lax.all_gather(own, ('dp', 'gx', 'core'), axis=0)  8.84 us
    all_to_all x1, blocking collectives, on_device(): own = jnp.sum(lax.all_to_all(column, 'gy', 0, 0).astype(F32), axis=0)  8.29 us
    pallas_call x1, Pallas kernels, on_device(): pl.pallas_call(functools.partial(early_kernel, (c1, c2, c3, depth, height...  5.05 us
    pallas_call x1, Pallas kernels, on_device(): pl.pallas_call(functools.partial(gather_kernel, (c1, depth, height, bread...  2.09 us
    ppermute x1, waiting for transfers between devices, on_device(): other = lax.ppermute(send, 'core', [(0, 1), (1, 0)])  1.97 us
    pallas_call x1, Pallas kernels, on_device(): pl.pallas_call(functools.partial(main_kernel, (c1, c2, c3, depth, height,...  1.82 us
  transfers between devices with their start and end apart: 5, of which 1 were waited for; matrix products, arithmetic and copies ran while one was open for 0% of the time, Pallas kernels for 13%

profile of v4, /device:TPU:0, one launch (start us, length us, event | category | flops | bytes accessed | tf_op | source)
XLA Modules:
  0.0 53.7 jit_solution(2732169802944987710)
XLA Ops:
  0.6 0.0 copy-start.2
  0.6 1.1 %pad_select_fusion = (bf16[32,16,256]{2,1,0:T(8,128)(2,1)S(1)}, bf16[32,16,256]{2,1,0:T(8,128)(2,1)S(1)}) fusion(bf16[32,16,128]{2,1,0:T(8,128)(2,1)} %bitcast.28, pred[]{:T(512)S(6)} %eq.3, bf16[32,128,256]{2,1,0:T(8,128)(2,1)} %bitcast.22), kind=kLoop, calls=%fused_computation.2 | loop fusion | flops 262144 | bytes 917505 | tf_op jit(solution)/shard_map/jit(_where)/select_n | solution.py:332
  1.8 0.7 %collective-permute-start.1 = (bf16[32,16,256]{2,1,0:T(8,128)(2,1)S(1)}, bf16[32,16,256]{2,1,0:T(8,128)(2,1)S(1)}, u32[]{:S(2)}, u32[]{:S(2)}) collective-permute-start(bf16[32,16,256]{2,1,0:T(8,128)(2,1)S(1)} %get-tuple-element.40), channel_id=1, source_target_pairs={{4,8},{8,4},{5,9},{9,5},{6,10},{10,6},{7,11},{11,7},{20,24},{24,20... | collective-permute-start | bytes 786440 | tf_op jit(solution)/shard_map/ppermute | solution.py:24
  2.5 4.3 %collective-permute-start = (bf16[32,16,256]{2,1,0:T(8,128)(2,1)S(1)}, bf16[32,16,256]{2,1,0:T(8,128)(2,1)S(1)}, u32[]{:S(2)}, u32[]{:S(2)}) collective-permute-start(bf16[32,16,256]{2,1,0:T(8,128)(2,1)S(1)} %get-tuple-element.41), channel_id=1, source_target_pairs={{0,4},{8,12},{4,0},{12,8},{1,5},{9,13},{5,1},{13,9},{2,6},{10,14},... | collective-permute-start | bytes 786440 | tf_op jit(solution)/shard_map/ppermute | solution.py:24
  6.8 0.0 copy-start
  6.8 1.6 %copy-done = bf16[1,32,8,16,256]{4,3,2,1,0:T(8,128)(2,1)S(1)} copy-done((bf16[1,32,8,16,256]{4,3,2,1,0:T(8,128)(2,1)S(1)}, bf16[1,32,8,16,256]{4,3,2,1,0:T(8,128)(2,1)}, u32[]{:S(2)}) %copy-start) | copy-done | bytes 2097176
  8.4 2.1 %shard_map.60 = (bf16[1536,512]{1,0:T(8,128)(2,1)S(1)}, bf16[1536,512]{1,0:T(8,128)(2,1)S(1)}) custom-call(bf16[32,8,16,256]{3,2,1,0:T(8,128)(2,1)S(1)} %bitcast.23), custom_call_target="tpu_custom_call" | custom-call | flops 805306368 | bytes 8388608 | tf_op jit(solution)/shard_map/pallas_call | solution.py:337
  10.5 0.0 copy-start.1
  10.5 0.0 copy-start.3
  10.5 0.0 collective-permute-done.1.z_cross
  10.5 0.0 collective-permute-done.z_pair
  10.6 0.0 copy-done.2
  10.6 0.2 shard_map.59
  10.8 0.7 %collective-permute-start.2 = (bf16[288,256]{1,0:T(8,128)(2,1)S(1)}, bf16[288,256]{1,0:T(8,128)(2,1)S(1)}, u32[]{:S(2)}, u32[]{:S(2)}) collective-permute-start(bf16[288,256]{1,0:T(8,128)(2,1)S(1)} %get-tuple-element.34), channel_id=1, source_target_pairs={{1,2},{2,1},{5,6},{6,5},{9,10},{10,9},{13,14},{14,13},{17,18},{18,... | collective-permute-start | bytes 442376 | tf_op jit(solution)/shard_map/ppermute | solution.py:24
  11.5 4.5 %collective-permute-start.3 = (bf16[288,256]{1,0:T(8,128)(2,1)S(1)}, bf16[288,256]{1,0:T(8,128)(2,1)S(1)}, u32[]{:S(2)}, u32[]{:S(2)}) collective-permute-start(bf16[288,256]{1,0:T(8,128)(2,1)S(1)} %get-tuple-element.35), channel_id=1, source_target_pairs={{0,1},{2,3},{1,0},{3,2},{4,5},{6,7},{5,4},{7,6},{8,9},{10,11},{9,8... | collective-permute-start | bytes 442376 | tf_op jit(solution)/shard_map/ppermute | solution.py:24
  15.9 0.0 copy-done.1
  16.0 0.0 copy-done.3
  16.0 5.1 %shard_map.61 = (bf16[1632,128]{1,0:T(8,128)(2,1)S(1)}, bf16[256,1024]{1,0:T(8,128)(2,1)S(1)}, f32[8,64,512]{2,1,0:T(8,128)S(1)}, bf16[1920,384]{1,0:T(8,128)(2,...) custom-call(bf16[1536,512]{1,0:T(8,128)(2,1)S(1)} %get-tuple-element.25.even, ...), custom_call_target="tpu_custom_call" | custom-call | flops 805306368 | bytes 8388608 | tf_op jit(solution)/shard_map/pallas_call | solution.py:370
  21.0 0.0 collective-permute-done.2.y_cross
  21.0 0.0 collective-permute-done.3.y_pair
  21.0 1.8 %shard_map.62 = (f32[1120,128]{1,0:T(8,128)S(1)}, f32[1120,128]{1,0:T(8,128)S(1)}) custom-call(bf16[1536,512]{1,0:T(8,128)(2,1)S(1)} %get-tuple-element.25.even, bf16[1536,512]{1,0:T(8,128)(2,1)S(1)} %get-tuple-element.26.odd, bf16[1632,128]{1,0:T(8,128)(2,1)S(1)} %get-tuple-element.27.rim_z, bf16[256,1024]{1,0:T(8,128)(2,1)S(1)} %get-tuple-element.28.act, ...), custom_call_target="tpu_custom_call" | custom-call | tf_op jit(solution)/shard_map/pallas_call | solution.py:393
  22.9 0.1 collective-permute-start.4
  22.9 2.0 %collective-permute-done.4 = f32[1120,128]{1,0:T(8,128)S(1)} collective-permute-done((f32[1120,128]{1,0:T(8,128)S(1)}, f32[1120,128]{1,0:T(8,128)S(1)}, u32[]{:S(2)}, u32[]{:S(2)}) %collective-permute-start.4) | collective-permute-done | bytes 573472 | tf_op jit(solution)/shard_map/ppermute | solution.py:411
  24.9 0.1 add_convert_fusion
  25.0 10.4 %all_to_all.10 = bf16[4,280,128]{2,1,0:T(8,128)(2,1)S(1)} all-to-all(bf16[4,280,128]{2,1,0:T(8,128)(2,1)S(1)} %bitcast.33), channel_id=1, replica_groups=mesh['dp'=2,'gx'=2,'core'=2,'gy'=4] {'dp','gx'}, dimensions={0} | all-to-all | bytes 573440 | tf_op jit(solution)/shard_map/all_to_all | solution.py:413
  35.5 8.3 %all_to_all.11 = bf16[4,112,128]{2,1,0:T(8,128)(2,1)S(1)} all-to-all(bf16[4,112,128]{2,1,0:T(8,128)(2,1)S(1)} %pad_maximum_fusion), channel_id=1, replica_groups=mesh['dp'=2,'gx'=2,'core'=2,'gy'=4] {'gy'}, dimensions={0} | all-to-all | bytes 229376 | tf_op jit(solution)/shard_map/all_to_all | solution.py:417
  43.8 8.8 %all-gather = f32[896,128]{1,0:T(8,128)S(1)} all-gather(f32[112,128]{1,0:T(8,128)S(1)} %convert_reduce_fusion.1), channel_id=2, replica_groups=mesh['dp'=2,'gx'=2,'core'=2,'gy'=4] {'dp','gx','core'}, dimensions={0}, use_global_device_ids=true | all-gather | bytes 516096 | tf_op jit(solution)/shard_map/all_gather | solution.py:418
  52.7 1.0 %shard_map.63 = (f32[864,64]{1,0:T(8,128)}, f32[27,32,64]{2,1,0:T(8,128)}) custom-call(f32[8,112,128]{2,1,0:T(8,128)S(1)} %bitcast.25), custom_call_target="tpu_custom_call" | custom-call | tf_op jit(solution)/shard_map/pallas_call | solution.py:420
  (6 shorter events, 0.1 us)
Async XLA Ops:
  0.6 9.9 %copy-start.2 = (bf16[1,128,2,4,64]{1,4,3,2,0:T(8,128)(2,1)S(1)}, bf16[1,128,2,4,64]{1,4,3,2,0:T(8,128)(2,1)}, u32[]{:S(2)}) copy-start(bf16[1,128,2,4,64]{1,4,3,2,0:T(8,128)(2,1)} %param.7) | copy-start | bytes 393220
  1.8 8.7 %collective-permute-start.1 = (bf16[32,16,256]{2,1,0:T(8,128)(2,1)S(1)}, bf16[32,16,256]{2,1,0:T(8,128)(2,1)S(1)}, u32[]{:S(2)}, u32[]{:S(2)}) collective-permute-start(bf16[32,16,256]{2,1,0:T(8,128)(2,1)S(1)} %get-tuple-element.40), channel_id=1, source_target_pairs={{4,8},{8,4},{5,9},{9,5},{6,10},{10,6},{7,11},{11,7},{20,24},{24,20... | collective-permute-start | bytes 786440 | tf_op jit(solution)/shard_map/ppermute | solution.py:24
  2.5 8.1 %collective-permute-start = (bf16[32,16,256]{2,1,0:T(8,128)(2,1)S(1)}, bf16[32,16,256]{2,1,0:T(8,128)(2,1)S(1)}, u32[]{:S(2)}, u32[]{:S(2)}) collective-permute-start(bf16[32,16,256]{2,1,0:T(8,128)(2,1)S(1)} %get-tuple-element.41), channel_id=1, source_target_pairs={{0,4},{8,12},{4,0},{12,8},{1,5},{9,13},{5,1},{13,9},{2,6},{10,14},... | collective-permute-start | bytes 786440 | tf_op jit(solution)/shard_map/ppermute | solution.py:24
  6.8 1.6 %copy-start = (bf16[1,32,8,16,256]{4,3,2,1,0:T(8,128)(2,1)S(1)}, bf16[1,32,8,16,256]{4,3,2,1,0:T(8,128)(2,1)}, u32[]{:S(2)}) copy-start(bf16[1,32,8,16,256]{4,3,2,1,0:T(8,128)(2,1)} %param.4) | copy-start | bytes 6291460
  10.5 5.4 %copy-start.1 = (bf16[128,64,3,3,3]{0,1,4,3,2:T(8,128)(2,1)S(1)}, bf16[128,64,3,3,3]{0,1,4,3,2:T(8,128)(2,1)}, u32[]{:S(2)}) copy-start(bf16[128,64,3,3,3]{0,1,4,3,2:T(8,128)(2,1)} %param.6) | copy-start | bytes 1327108
  10.5 5.4 %copy-start.3 = (bf16[64,32,3,3,3]{0,1,4,3,2:T(8,128)(2,1)S(1)}, bf16[64,32,3,3,3]{0,1,4,3,2:T(8,128)(2,1)}, u32[]{:S(2)}) copy-start(bf16[64,32,3,3,3]{0,1,4,3,2:T(8,128)(2,1)} %param.5) | copy-start | bytes 331780
  10.8 10.2 %collective-permute-start.2 = (bf16[288,256]{1,0:T(8,128)(2,1)S(1)}, bf16[288,256]{1,0:T(8,128)(2,1)S(1)}, u32[]{:S(2)}, u32[]{:S(2)}) collective-permute-start(bf16[288,256]{1,0:T(8,128)(2,1)S(1)} %get-tuple-element.34), channel_id=1, source_target_pairs={{1,2},{2,1},{5,6},{6,5},{9,10},{10,9},{13,14},{14,13},{17,18},{18,... | collective-permute-start | bytes 442376 | tf_op jit(solution)/shard_map/ppermute | solution.py:24
  11.5 9.5 %collective-permute-start.3 = (bf16[288,256]{1,0:T(8,128)(2,1)S(1)}, bf16[288,256]{1,0:T(8,128)(2,1)S(1)}, u32[]{:S(2)}, u32[]{:S(2)}) collective-permute-start(bf16[288,256]{1,0:T(8,128)(2,1)S(1)} %get-tuple-element.35), channel_id=1, source_target_pairs={{0,1},{2,3},{1,0},{3,2},{4,5},{6,7},{5,4},{7,6},{8,9},{10,11},{9,8... | collective-permute-start | bytes 442376 | tf_op jit(solution)/shard_map/ppermute | solution.py:24
  22.9 2.0 %collective-permute-start.4 = (f32[1120,128]{1,0:T(8,128)S(1)}, f32[1120,128]{1,0:T(8,128)S(1)}, u32[]{:S(2)}, u32[]{:S(2)}) collective-permute-start(f32[1120,128]{1,0:T(8,128)S(1)} %get-tuple-element.37), channel_id=1, source_target_pairs={{0,4},{4,0},{1,5},{5,1},{2,6},{6,2},{3,7},{7,3},{8,12},{12,8},{9,1... | collective-permute-start | bytes 1720328 | tf_op jit(solution)/shard_map/ppermute | solution.py:411

commit v5 on v4

--- a/solution.py
+++ b/solution.py
@@ -99,6 +99,30 @@
         spread_layer(rows, pick, tall.at[layer % 2], turned.at[layer % 2], height, put)
 
 
+def back_kernel(cot, kd, order, pairs, back):
+    dz, dy, dx, c3 = cot.shape
+    c2, mx = kd.shape[1], 2 * dx
+    last = lax.broadcasted_iota(jnp.int32, (dx, c3), 0) == dx - 1
+    for z in range(dz):
+        for y in range(dy):
+            put_pair(pairs, (z * dy + y) * mx, cot[z, y], last)
+    for sy in range(2):
+        classes, taps = classes_of(0, sy)
+        filters = filters_of(kd, taps)
+        for z in range(dz):
+            start, count = z * dy * mx, (dy - sy) * mx
+            add_grads(back, dot(filters, pairs[start + sy * mx : start + dy * mx, :], NT), classes, start, count, c2, sy)
+
+
+def add_grads(back, grads, classes, start, count, c2, held):
+    for n, (pz, py) in enumerate(classes):
+        rows = slice((pz * 2 + py) * c2, (pz * 2 + py + 1) * c2)
+        piece = grads[n * c2 : (n + 1) * c2]
+        if held:
+            piece = piece + back[rows, start : start + count]
+        back[rows, start : start + count] = piece
+
+
 def silu_and_slope(pre):
     sigma = jax.nn.sigmoid(pre)
     return (pre * sigma).astype(BF16), sigma * (1.0 + pre * (1.0 - sigma))
@@ -137,7 +161,7 @@
     return odd[rows, :] if az == 1 else even[rows, :]
 
 
-def early_kernel(dims, even, odd, z_pair, z_cross, cot, km, kd, rim_z, act, slope, pairs, back, deep, mid, below, above, tall, turned, grad):
+def early_kernel(dims, even, odd, pairs, back_in, z_pair, z_cross, km, kd, rim_z, act, slope, pairs_above, back, deep, mid, below, above, tall, turned, grad):
     c1, c2, c3, depth, height, breadth = dims
     mz, my, mx = depth // 2, height // 2, breadth // 2
     dz, dy, dx = mz // 2, my // 2, mx // 2
@@ -158,9 +182,9 @@
         put_active(act, active, y, c2, dy, mx)
 
     last = lax.broadcasted_iota(jnp.int32, (dx, c3), 0) == dx - 1
-    for z in range(dz + 1):
-        for y in range(dy):
-            put_pair(pairs, (z * (dy + 1) + y) * mx, above[y] if z == dz else cot[z, y], last)
+    for y in range(dy):
+        put_pair(pairs_above, y * mx, above[y], last)
+    back[...] = back_in[...]
 
     for sz in range(2):
         for sy in range(2):
@@ -170,17 +194,14 @@
             total = None
             for z in range(dz):
                 start, count = z * dy * mx, (dy - sy) * mx
-                top = ((z + sz) * (dy + 1) + sy) * mx
-                cells = pairs[top : top + count, :]
+                source, first = (pairs, start) if z + sz < dz else (pairs_above, 0)
+                if sz and source is pairs:
+                    first = (z + sz) * dy * mx
+                cells = source[first + sy * mx : first + dy * mx, :]
                 term = dot(lhs[:, start : start + count], cells)
                 total = term if total is None else total + term
-                grads = dot(filters, cells, NT)
-                for n, (pz, py) in enumerate(classes):
-                    rows = slice((pz * 2 + py) * c2, (pz * 2 + py + 1) * c2)
-                    piece = grads[n * c2 : (n + 1) * c2]
-                    if sz or sy:
-                        piece = piece + back[rows, start : start + count]
-                    back[rows, start : start + count] = piece
+                if sz:
+                    add_grads(back, dot(filters, cells, NT), classes, start, count, c2, True)
             for n, (az, ay) in enumerate(taps):
                 deep[az * 3 + ay] = total[n * c2 : (n + 1) * c2]
 
@@ -202,7 +223,7 @@
         dst[:, z * mx : (z + 1) * mx] = value.astype(BF16)
 
 
-def main_kernel(dims, even, odd, rim_z, act, slope, pairs, back_in, deep_in, mid_in, y_cross, y_pair, km, kd, keep, send, beside, cot_beside, corner, rim_even, rim_odd, rim_pairs, back, grad, sums):
+def main_kernel(dims, even, odd, rim_z, act, slope, pairs, pairs_above, back_in, deep_in, mid_in, y_cross, y_pair, km, kd, keep, send, beside, cot_beside, corner, rim_even, rim_odd, rim_pairs, back, grad, sums):
     c1, c2, c3, depth, height, breadth, n_pl, n_gy = dims
     mz, my, mx = depth // 2, height // 2, breadth // 2
     dz, dy, dx = mz // 2, my // 2, mx // 2
@@ -253,8 +274,8 @@
                     for n, r in enumerate(rows):
                         back[r, lanes] = back[r, lanes] + grads[n * c2 : (n + 1) * c2]
                 else:
-                    top = (z + sz) * (dy + 1) * mx
-                    cells = pairs[top : top + mx, :]
+                    top = (z + sz) * dy * mx
+                    cells = pairs[top : top + mx, :] if z + sz < dz else pairs_above[:mx, :]
                     lhs = [active[:, (2 * z + pz) * mx : (2 * z + pz + 1) * mx] for (pz, py), _ in group]
                 term = dot(jnp.concatenate(lhs, axis=0), cells)
                 for n, (_, tap) in enumerate(group):
@@ -334,6 +355,9 @@
     z_pair = swapped(pair, gz, 0)
     blk = 3 * c1
     own_cells = jax.ShapeDtypeStruct((height * blk, mz * mx), BF16)
+    km = kernel_mid.transpose(2, 3, 4, 1, 0).reshape(27 * c1, c2)
+    kd = kernel_deep.transpose(2, 3, 4, 1, 0).reshape(27, c2, c3)
+    back_shape = jax.ShapeDtypeStruct((4 * c2, dz * dy * mx), F32)
     even, odd = pl.pallas_call(
         functools.partial(gather_kernel, (c1, depth, height, breadth)),
         out_shape=(own_cells, own_cells),
@@ -346,6 +370,14 @@
         cost_estimate=pl.CostEstimate(flops=2 * c1 * depth * height * breadth * 3 * mx, bytes_accessed=8 << 20, transcendentals=0),
         compiler_params=pltpu.CompilerParams(vmem_limit_bytes=24 * 1024 * 1024),
     )(vol)
+    pairs, back = pl.pallas_call(
+        back_kernel,
+        out_shape=(jax.ShapeDtypeStruct((dz * dy * mx, 3 * c3), BF16), back_shape),
+        in_specs=[in_vmem] * 3,
+        out_specs=(in_vmem, in_vmem),
+        cost_estimate=pl.CostEstimate(flops=2 * 27 * c2 * c3 * dz * dy * dx, bytes_accessed=2 << 20, transcendentals=0),
+        compiler_params=pltpu.CompilerParams(vmem_limit_bytes=16 * 1024 * 1024),
+    )(cot, kd, odd)
     payload = jax.ShapeDtypeStruct(((depth + 1) * c1, breadth), BF16)
     pair, cross = pl.pallas_call(
         functools.partial(edge_kernel, (c1, depth, height, breadth)),
@@ -359,26 +391,24 @@
         ],
         compiler_params=pltpu.CompilerParams(vmem_limit_bytes=16 * 1024 * 1024),
     )(vol, cot, z_pair, z_cross)
-    pair, cross, even, odd = lax.optimization_barrier((pair, cross, even, odd))
+    pair, cross, even, odd, pairs, back = lax.optimization_barrier((pair, cross, even, odd, pairs, back))
     y_pair, y_cross = swapped(pair, "gy", 0), swapped(cross, "gy", 1)
-    km = kernel_mid.transpose(2, 3, 4, 1, 0).reshape(27 * c1, c2)
-    kd = kernel_deep.transpose(2, 3, 4, 1, 0).reshape(27, c2, c3)
 
     share = c3 // n_gy
     per = 448 // (2 * n_pl)
     chunk = (n_gy + 1) * per
-    rim_z, act, slope, pairs, back, deep, mid = pl.pallas_call(
+    rim_z, act, slope, pairs_above, back, deep, mid = pl.pallas_call(
         functools.partial(early_kernel, (c1, c2, c3, depth, height, breadth)),
         out_shape=(
             jax.ShapeDtypeStruct(((height + 1) * blk, mx), BF16),
             jax.ShapeDtypeStruct((4 * c2, dz * dy * mx), BF16),
             jax.ShapeDtypeStruct((my, c2, mz * mx), F32),
-            jax.ShapeDtypeStruct(((dz + 1) * (dy + 1) * mx, 3 * c3), BF16),
-            jax.ShapeDtypeStruct((4 * c2, dz * dy * mx), F32),
+            jax.ShapeDtypeStruct((dy * mx, 3 * c3), BF16),
+            back_shape,
             jax.ShapeDtypeStruct((9, c2, 3 * c3), F32),
             jax.ShapeDtypeStruct((3, 3 * blk, c2), F32),
         ),
-        in_specs=[in_vmem] * 7,
+        in_specs=[in_vmem] * 8,
         out_specs=(in_vmem,) * 7,
         scratch_shapes=[
             pltpu.VMEM((c1 * height, breadth), BF16),
@@ -389,11 +419,11 @@
         ],
         cost_estimate=pl.CostEstimate(flops=2 * c1 * depth * height * breadth * 3 * mx, bytes_accessed=8 << 20, transcendentals=0),
         compiler_params=pltpu.CompilerParams(vmem_limit_bytes=24 * 1024 * 1024),
-    )(even, odd, z_pair, z_cross, cot, km, kd)
+    )(even, odd, pairs, back, z_pair, z_cross, km, kd)
     keep, send = pl.pallas_call(
         functools.partial(main_kernel, (c1, c2, c3, depth, height, breadth, n_pl, n_gy)),
         out_shape=(jax.ShapeDtypeStruct((n_pl * chunk, 128), F32), jax.ShapeDtypeStruct((n_pl * chunk, 128), F32)),
-        in_specs=[in_vmem] * 13,
+        in_specs=[in_vmem] * 14,
         out_specs=(in_vmem, in_vmem),
         scratch_shapes=[
             pltpu.VMEM(((depth + 1) * c1, breadth), BF16),
@@ -407,7 +437,7 @@
             pltpu.VMEM((2, n_pl * chunk, 128), F32),
         ],
         compiler_params=pltpu.CompilerParams(vmem_limit_bytes=32 * 1024 * 1024),
-    )(even, odd, rim_z, act, slope, pairs, back, deep, mid, y_cross, y_pair, km, kd)
+    )(even, odd, rim_z, act, slope, pairs, pairs_above, back, deep, mid, y_cross, y_pair, km, kd)
     other = lax.ppermute(send, "core", [(0, 1), (1, 0)])
     pair = (keep + other).astype(BF16).reshape(n_pl, chunk, 128)
     own = jnp.sum(lax.all_to_all(pair, ("dp", "gx"), 0, 0).astype(F32), axis=0)

time: 54 us -> 53.2 us (0.985)
  blocking collectives: 27.6 us -> 26.9 us
    pallas_call x1, Pallas kernels: 5.05 us -> 4.25 us  [on_device(): pl.pallas_call(functools.partial(early_kernel, (c1, c2, c3, depth, height...]
    all_to_all x1, blocking collectives: 10.4 us -> 9.8 us  [on_device(): own = jnp.sum(lax.all_to_all(pair, ('dp', 'gx'), 0, 0).astype(F32), axis=0)]
    pallas_call x0 -> x1, Pallas kernels: none -> 0.63 us  [on_device(): pl.pallas_call(back_kernel, out_shape=(jax.ShapeDtypeStruct((dz * dy * mx...]
where the time goes in v5:
time: 53.2 us; the launch traced here: 53 us
  blocking collectives  26.9 us (51%)
  starting transfers between devices  10.2 us (19%)
  Pallas kernels  10.1 us (19%)
  waiting for transfers between devices  1.98 us (4%)
  local copies, waits for them, and re-layouts  1.62 us (3%)
  other arithmetic  1.31 us (2%)
  between operations  0.8 us (2%)
    ppermute x4, starting transfers between devices, swapped(): return lax.ppermute(block, axis, route + [(j, i) for i, j in route])  10.1 us
    all_to_all x1, blocking collectives, on_device(): own = jnp.sum(lax.all_to_all(pair, ('dp', 'gx'), 0, 0).astype(F32), axis=0)  9.8 us
    all_gather x1, blocking collectives, on_device(): whole = lax.all_gather(own, ('dp', 'gx', 'core'), axis=0)  8.84 us
    all_to_all x1, blocking collectives, on_device(): own = jnp.sum(lax.all_to_all(column, 'gy', 0, 0).astype(F32), axis=0)  8.3 us
    pallas_call x1, Pallas kernels, on_device(): pl.pallas_call(functools.partial(early_kernel, (c1, c2, c3, depth, height...  4.25 us
    pallas_call x1, Pallas kernels, on_device(): pl.pallas_call(functools.partial(gather_kernel, (c1, depth, height, bread...  2.08 us
    ppermute x1, waiting for transfers between devices, on_device(): other = lax.ppermute(send, 'core', [(0, 1), (1, 0)])  1.97 us
    pallas_call x1, Pallas kernels, on_device(): pl.pallas_call(functools.partial(main_kernel, (c1, c2, c3, depth, height,...  1.83 us
  transfers between devices with their start and end apart: 5, of which 1 were waited for; matrix products, arithmetic and copies ran while one was open for 0% of the time, Pallas kernels for 13%

profile of v5, /device:TPU:0, one launch (start us, length us, event | category | flops | bytes accessed | tf_op | source)
XLA Modules:
  0.0 53.0 jit_solution(6451606664579872932)
XLA Ops:
  0.6 0.0 copy-start.2
  0.6 0.0 copy-start
  0.7 1.2 %pad_select_fusion = (bf16[32,16,256]{2,1,0:T(8,128)(2,1)S(1)}, bf16[32,16,256]{2,1,0:T(8,128)(2,1)S(1)}) fusion(bf16[32,16,128]{2,1,0:T(8,128)(2,1)} %bitcast.29, pred[]{:T(512)S(6)} %eq.3, bf16[32,128,256]{2,1,0:T(8,128)(2,1)} %bitcast.25), kind=kLoop, calls=%fused_computation.2 | loop fusion | flops 262144 | bytes 917505 | tf_op jit(solution)/shard_map/jit(_where)/select_n | solution.py:353
  1.8 0.7 %collective-permute-start.1 = (bf16[32,16,256]{2,1,0:T(8,128)(2,1)S(1)}, bf16[32,16,256]{2,1,0:T(8,128)(2,1)S(1)}, u32[]{:S(2)}, u32[]{:S(2)}) collective-permute-start(bf16[32,16,256]{2,1,0:T(8,128)(2,1)S(1)} %get-tuple-element.48), channel_id=1, source_target_pairs={{4,8},{8,4},{5,9},{9,5},{6,10},{10,6},{7,11},{11,7},{20,24},{24,20... | collective-permute-start | bytes 786440 | tf_op jit(solution)/shard_map/ppermute | solution.py:24
  2.5 4.3 %collective-permute-start = (bf16[32,16,256]{2,1,0:T(8,128)(2,1)S(1)}, bf16[32,16,256]{2,1,0:T(8,128)(2,1)S(1)}, u32[]{:S(2)}, u32[]{:S(2)}) collective-permute-start(bf16[32,16,256]{2,1,0:T(8,128)(2,1)S(1)} %get-tuple-element.49), channel_id=1, source_target_pairs={{0,4},{8,12},{4,0},{12,8},{1,5},{9,13},{5,1},{13,9},{2,6},{10,14},... | collective-permute-start | bytes 786440 | tf_op jit(solution)/shard_map/ppermute | solution.py:24
  6.9 0.0 copy-start.1
  6.9 1.6 %copy-done.1 = bf16[1,32,8,16,256]{4,3,2,1,0:T(8,128)(2,1)S(1)} copy-done((bf16[1,32,8,16,256]{4,3,2,1,0:T(8,128)(2,1)S(1)}, bf16[1,32,8,16,256]{4,3,2,1,0:T(8,128)(2,1)}, u32[]{:S(2)}) %copy-start.1) | copy-done | bytes 2097176
  8.4 2.1 %shard_map.60 = (bf16[1536,512]{1,0:T(8,128)(2,1)S(1)}, bf16[1536,512]{1,0:T(8,128)(2,1)S(1)}) custom-call(bf16[32,8,16,256]{3,2,1,0:T(8,128)(2,1)S(1)} %bitcast.26), custom_call_target="tpu_custom_call" | custom-call | flops 805306368 | bytes 8388608 | tf_op jit(solution)/shard_map/pallas_call | solution.py:361
  10.5 0.0 copy-done.2
  10.5 0.0 copy-done
  10.6 0.0 copy-start.3
  10.6 0.6 %shard_map.61 = (bf16[1024,384]{1,0:T(8,128)(2,1)S(1)}, f32[256,1024]{1,0:T(8,128)S(1)}) custom-call(bf16[2,4,64,128]{3,2,1,0:T(8,128)(2,1)S(1)} %bitcast.30, bf16[27,64,128]{2,1,0:T(8,128)(2,1)S(1)} %bitcast.22, bf16[1536,512]{1,0:T(8,128)(2,1)S(1)} %get-tuple-element.32.order.odd), custom_call_target="tpu_custom_call" | custom-call | flops 226492416 | bytes 2097152 | tf_op jit(solution)/shard_map/pallas_call | solution.py:373
  11.2 0.0 collective-permute-done.1.z_cross
  11.2 0.0 collective-permute-done.z_pair
  11.2 0.3 shard_map.59
  11.5 0.7 %collective-permute-start.2 = (bf16[288,256]{1,0:T(8,128)(2,1)S(1)}, bf16[288,256]{1,0:T(8,128)(2,1)S(1)}, u32[]{:S(2)}, u32[]{:S(2)}) collective-permute-start(bf16[288,256]{1,0:T(8,128)(2,1)S(1)} %get-tuple-element.42), channel_id=1, source_target_pairs={{1,2},{2,1},{5,6},{6,5},{9,10},{10,9},{13,14},{14,13},{17,18},{18,... | collective-permute-start | bytes 442376 | tf_op jit(solution)/shard_map/ppermute | solution.py:24
  12.2 4.5 %collective-permute-start.3 = (bf16[288,256]{1,0:T(8,128)(2,1)S(1)}, bf16[288,256]{1,0:T(8,128)(2,1)S(1)}, u32[]{:S(2)}, u32[]{:S(2)}) collective-permute-start(bf16[288,256]{1,0:T(8,128)(2,1)S(1)} %get-tuple-element.43), channel_id=1, source_target_pairs={{0,1},{2,3},{1,0},{3,2},{4,5},{6,7},{5,4},{7,6},{8,9},{10,11},{9,8... | collective-permute-start | bytes 442376 | tf_op jit(solution)/shard_map/ppermute | solution.py:24
  16.6 0.0 copy-done.3
  16.6 4.2 %shard_map.62 = (bf16[1632,128]{1,0:T(8,128)(2,1)S(1)}, bf16[256,1024]{1,0:T(8,128)(2,1)S(1)}, f32[8,64,512]{2,1,0:T(8,128)S(1)}, bf16[512,384]{1,0:T(8,128)(2,1...) custom-call(bf16[1536,512]{1,0:T(8,128)(2,1)S(1)} %get-tuple-element.31.even, ...), custom_call_target="tpu_custom_call" | custom-call | flops 805306368 | bytes 8388608 | tf_op jit(solution)/shard_map/pallas_call | solution.py:400
  20.9 0.0 collective-permute-done.2.y_cross
  20.9 0.0 collective-permute-done.3.y_pair
  20.9 1.8 %shard_map.63 = (f32[1120,128]{1,0:T(8,128)S(1)}, f32[1120,128]{1,0:T(8,128)S(1)}) custom-call(bf16[1536,512]{1,0:T(8,128)(2,1)S(1)} %get-tuple-element.31.even, bf16[1536,512]{1,0:T(8,128)(2,1)S(1)} %get-tuple-element.32.order.odd, bf16[1632,128]{1,0:T(8,128)(2,1)S(1)} %get-tuple-element.35.rim_z, bf16[256,1024]{1,0:T(8,128)(2,1)S(1)} %get-tuple-element.36.act, ...), custom_call_target="tpu_custom_call" | custom-call | tf_op jit(solution)/shard_map/pallas_call | solution.py:423
  22.7 0.1 collective-permute-start.4
  22.8 2.0 %collective-permute-done.4 = f32[1120,128]{1,0:T(8,128)S(1)} collective-permute-done((f32[1120,128]{1,0:T(8,128)S(1)}, f32[1120,128]{1,0:T(8,128)S(1)}, u32[]{:S(2)}, u32[]{:S(2)}) %collective-permute-start.4) | collective-permute-done | bytes 573472 | tf_op jit(solution)/shard_map/ppermute | solution.py:441
  24.8 0.1 add_convert_fusion
  24.9 9.8 %all_to_all.10 = bf16[4,280,128]{2,1,0:T(8,128)(2,1)S(1)} all-to-all(bf16[4,280,128]{2,1,0:T(8,128)(2,1)S(1)} %bitcast.34), channel_id=1, replica_groups=mesh['dp'=2,'gx'=2,'core'=2,'gy'=4] {'dp','gx'}, dimensions={0} | all-to-all | bytes 573440 | tf_op jit(solution)/shard_map/all_to_all | solution.py:443
  34.8 8.3 %all_to_all.11 = bf16[4,112,128]{2,1,0:T(8,128)(2,1)S(1)} all-to-all(bf16[4,112,128]{2,1,0:T(8,128)(2,1)S(1)} %pad_maximum_fusion), channel_id=1, replica_groups=mesh['dp'=2,'gx'=2,'core'=2,'gy'=4] {'gy'}, dimensions={0} | all-to-all | bytes 229376 | tf_op jit(solution)/shard_map/all_to_all | solution.py:447
  43.1 8.8 %all-gather = f32[896,128]{1,0:T(8,128)S(1)} all-gather(f32[112,128]{1,0:T(8,128)S(1)} %convert_reduce_fusion.1), channel_id=2, replica_groups=mesh['dp'=2,'gx'=2,'core'=2,'gy'=4] {'dp','gx','core'}, dimensions={0}, use_global_device_ids=true | all-gather | bytes 516096 | tf_op jit(solution)/shard_map/all_gather | solution.py:448
  51.9 1.0 %shard_map.64 = (f32[864,64]{1,0:T(8,128)}, f32[27,32,64]{2,1,0:T(8,128)}) custom-call(f32[8,112,128]{2,1,0:T(8,128)S(1)} %bitcast.28), custom_call_target="tpu_custom_call" | custom-call | tf_op jit(solution)/shard_map/pallas_call | solution.py:450
  (6 shorter events, 0.1 us)
Async XLA Ops:
  0.6 9.9 %copy-start.2 = (bf16[1,128,2,4,64]{1,4,3,2,0:T(8,128)(2,1)S(1)}, bf16[1,128,2,4,64]{1,4,3,2,0:T(8,128)(2,1)}, u32[]{:S(2)}) copy-start(bf16[1,128,2,4,64]{1,4,3,2,0:T(8,128)(2,1)} %param.7) | copy-start | bytes 393220
  0.6 9.9 %copy-start = (bf16[128,64,3,3,3]{0,1,4,3,2:T(8,128)(2,1)S(1)}, bf16[128,64,3,3,3]{0,1,4,3,2:T(8,128)(2,1)}, u32[]{:S(2)}) copy-start(bf16[128,64,3,3,3]{0,1,4,3,2:T(8,128)(2,1)} %param.6) | copy-start | bytes 1327108
  1.8 9.4 %collective-permute-start.1 = (bf16[32,16,256]{2,1,0:T(8,128)(2,1)S(1)}, bf16[32,16,256]{2,1,0:T(8,128)(2,1)S(1)}, u32[]{:S(2)}, u32[]{:S(2)}) collective-permute-start(bf16[32,16,256]{2,1,0:T(8,128)(2,1)S(1)} %get-tuple-element.48), channel_id=1, source_target_pairs={{4,8},{8,4},{5,9},{9,5},{6,10},{10,6},{7,11},{11,7},{20,24},{24,20... | collective-permute-start | bytes 786440 | tf_op jit(solution)/shard_map/ppermute | solution.py:24
  2.5 8.7 %collective-permute-start = (bf16[32,16,256]{2,1,0:T(8,128)(2,1)S(1)}, bf16[32,16,256]{2,1,0:T(8,128)(2,1)S(1)}, u32[]{:S(2)}, u32[]{:S(2)}) collective-permute-start(bf16[32,16,256]{2,1,0:T(8,128)(2,1)S(1)} %get-tuple-element.49), channel_id=1, source_target_pairs={{0,4},{8,12},{4,0},{12,8},{1,5},{9,13},{5,1},{13,9},{2,6},{10,14},... | collective-permute-start | bytes 786440 | tf_op jit(solution)/shard_map/ppermute | solution.py:24
  6.9 1.6 %copy-start.1 = (bf16[1,32,8,16,256]{4,3,2,1,0:T(8,128)(2,1)S(1)}, bf16[1,32,8,16,256]{4,3,2,1,0:T(8,128)(2,1)}, u32[]{:S(2)}) copy-start(bf16[1,32,8,16,256]{4,3,2,1,0:T(8,128)(2,1)} %param.4) | copy-start | bytes 6291460
  10.6 6.1 %copy-start.3 = (bf16[64,32,3,3,3]{0,1,4,3,2:T(8,128)(2,1)S(1)}, bf16[64,32,3,3,3]{0,1,4,3,2:T(8,128)(2,1)}, u32[]{:S(2)}) copy-start(bf16[64,32,3,3,3]{0,1,4,3,2:T(8,128)(2,1)} %param.5) | copy-start | bytes 331780
  11.5 9.4 %collective-permute-start.2 = (bf16[288,256]{1,0:T(8,128)(2,1)S(1)}, bf16[288,256]{1,0:T(8,128)(2,1)S(1)}, u32[]{:S(2)}, u32[]{:S(2)}) collective-permute-start(bf16[288,256]{1,0:T(8,128)(2,1)S(1)} %get-tuple-element.42), channel_id=1, source_target_pairs={{1,2},{2,1},{5,6},{6,5},{9,10},{10,9},{13,14},{14,13},{17,18},{18,... | collective-permute-start | bytes 442376 | tf_op jit(solution)/shard_map/ppermute | solution.py:24
  12.2 8.7 %collective-permute-start.3 = (bf16[288,256]{1,0:T(8,128)(2,1)S(1)}, bf16[288,256]{1,0:T(8,128)(2,1)S(1)}, u32[]{:S(2)}, u32[]{:S(2)}) collective-permute-start(bf16[288,256]{1,0:T(8,128)(2,1)S(1)} %get-tuple-element.43), channel_id=1, source_target_pairs={{0,1},{2,3},{1,0},{3,2},{4,5},{6,7},{5,4},{7,6},{8,9},{10,11},{9,8... | collective-permute-start | bytes 442376 | tf_op jit(solution)/shard_map/ppermute | solution.py:24
  22.7 2.0 %collective-permute-start.4 = (f32[1120,128]{1,0:T(8,128)S(1)}, f32[1120,128]{1,0:T(8,128)S(1)}, u32[]{:S(2)}, u32[]{:S(2)}) collective-permute-start(f32[1120,128]{1,0:T(8,128)S(1)} %get-tuple-element.45), channel_id=1, source_target_pairs={{0,4},{4,0},{1,5},{5,1},{2,6},{6,2},{3,7},{7,3},{8,12},{12,8},{9,1... | collective-permute-start | bytes 1720328 | tf_op jit(solution)/shard_map/ppermute | solution.py:441

commit v6 on v5

--- a/solution.py
+++ b/solution.py
@@ -45,7 +45,7 @@
     c1 = rows.shape[0] // height
     rows = rows.astype(F32)
     for part in range(tall.shape[0]):
-        tall[part] = rows[:, part * 128 : (part + 1) * 128]
+        tall[part, : c1 * height] = rows[:, part * 128 : (part + 1) * 128]
     for y in range(height):
         parts = [tall[part, pl.ds(y, c1, stride=height), :] for part in range(tall.shape[0])]
         turned[y * c1 : (y + 1) * c1, :] = jnp.concatenate(parts, axis=1).astype(BF16)
@@ -78,7 +78,7 @@
             for part in range(breadth // 128):
                 lanes = slice(part * 128, (part + 1) * 128)
                 slot = (z * (breadth // 128) + part) % 4
-                tall[slot] = top[:, lanes]
+                tall[slot, : c1 * 8] = top[:, lanes]
                 up[z * c1 : (z + 1) * c1, lanes] = tall[slot, pl.ds(7, c1, stride=8), :].astype(BF16)
         for z in range(dz):
             down[z * dx : (z + 1) * dx, :c3] = cot[z, 0]
@@ -161,7 +161,7 @@
     return odd[rows, :] if az == 1 else even[rows, :]
 
 
-def early_kernel(dims, even, odd, pairs, back_in, z_pair, z_cross, km, kd, rim_z, act, slope, pairs_above, back, deep, mid, below, above, tall, turned, grad):
+def early_kernel(dims, even, odd, pairs, back_in, z_pair, z_cross, km, kd, rim_z, act, slope, pairs_above, back, deep, mid, turned_km, below, above, tall, turned, grad):
     c1, c2, c3, depth, height, breadth = dims
     mz, my, mx = depth // 2, height // 2, breadth // 2
     dz, dy, dx = mz // 2, my // 2, mx // 2
@@ -174,11 +174,11 @@
     by_parity("core", take, z_pair, z_cross)
     put = lambda y, piece: place(rim_z, (y + 1) * blk, slice(0, mx), piece)
     spread_layer(below[...], picking_matrix(breadth), tall, turned, height, put)
-    turned_km = km[...].astype(F32).T.astype(BF16)
+    turned_km[...] = km[...].astype(F32).T.astype(BF16)
     put_active(act, jnp.zeros((c2, mz * mx), BF16), 0, c2, dy, mx)
     for y in range(1, my):
         cells = jnp.concatenate([window(even, odd, rim_z, y, az, blk, mx) for az in range(3)], axis=0)
-        active, slope[y] = silu_and_slope(dot(turned_km, cells))
+        active, slope[y] = silu_and_slope(dot(turned_km[...], cells))
         put_active(act, active, y, c2, dy, mx)
 
     last = lax.broadcasted_iota(jnp.int32, (dx, c3), 0) == dx - 1
@@ -223,7 +223,7 @@
         dst[:, z * mx : (z + 1) * mx] = value.astype(BF16)
 
 
-def main_kernel(dims, even, odd, rim_z, act, slope, pairs, pairs_above, back_in, deep_in, mid_in, y_cross, y_pair, km, kd, keep, send, beside, cot_beside, corner, rim_even, rim_odd, rim_pairs, back, grad, sums):
+def main_kernel(dims, even, odd, rim_z, act, slope, pairs, pairs_above, back_in, deep_in, mid_in, y_cross, y_pair, turned_km, kd, keep, send, beside, cot_beside, corner, rim_even, rim_odd, rim_pairs, top, grad, sums):
     c1, c2, c3, depth, height, breadth, n_pl, n_gy = dims
     mz, my, mx = depth // 2, height // 2, breadth // 2
     dz, dy, dx = mz // 2, my // 2, mx // 2
@@ -251,14 +251,12 @@
         upper,
     ]
 
-    turned_km = km[...].astype(F32).T.astype(BF16)
-    active, low_slope = silu_and_slope(dot(turned_km, jnp.concatenate(first, axis=0)))
+    active, low_slope = silu_and_slope(dot(turned_km[...], jnp.concatenate(first, axis=0)))
 
     last = lax.broadcasted_iota(jnp.int32, (dx, c3), 0) == dx - 1
     for z in range(dz + 1):
         put_pair(rim_pairs, z * mx, cot_beside[z * dx : (z + 1) * dx, :], last)
 
-    back[...] = back_in[...]
     deep = {(az, ay): deep_in[az * 3 + ay] for az in range(3) for ay in range(3)}
     for sz in range(2):
         for sy in range(2):
@@ -271,11 +269,12 @@
                     cells = rim_pairs[(z + sz) * mx : (z + sz + 1) * mx, :]
                     lhs = [act[r, lanes] for r in rows]
                     grads = dot(filters, cells, NT)
-                    for n, r in enumerate(rows):
-                        back[r, lanes] = back[r, lanes] + grads[n * c2 : (n + 1) * c2]
+                    for n, ((pz, py), _) in enumerate(group):
+                        held = top[2 * z + pz] if sz else back_in[rows[n], lanes]
+                        top[2 * z + pz] = held + grads[n * c2 : (n + 1) * c2]
                 else:
-                    top = (z + sz) * dy * mx
-                    cells = pairs[top : top + mx, :] if z + sz < dz else pairs_above[:mx, :]
+                    start = (z + sz) * dy * mx
+                    cells = pairs[start : start + mx, :] if z + sz < dz else pairs_above[:mx, :]
                     lhs = [active[:, (2 * z + pz) * mx : (2 * z + pz + 1) * mx] for (pz, py), _ in group]
                 term = dot(jnp.concatenate(lhs, axis=0), cells)
                 for n, (_, tap) in enumerate(group):
@@ -285,8 +284,10 @@
         for az in range(3) for ay in range(3) for ax in range(3)
     }
 
-    put_grad(grad.at[0], back, low_slope, 0, c2, dy, mx)
-    put_grad(grad.at[1], back, slope[my - 1], my - 1, c2, dy, mx)
+    put_grad(grad.at[0], back_in, low_slope, 0, c2, dy, mx)
+    for z in range(mz):
+        lanes = slice(z * mx, (z + 1) * mx)
+        grad[1, :, lanes] = (top[z] * slope[my - 1, :, lanes]).astype(BF16)
     mids = []
     for az in range(3):
         upper_row = dot(window(even, odd, rim_z, my - 1, az, blk, mx), grad[1], NT)
@@ -364,7 +365,7 @@
         in_specs=[in_vmem],
         out_specs=(in_vmem, in_vmem),
         scratch_shapes=[
-            pltpu.VMEM((2, breadth // 128, c1 * height, 128), F32),
+            pltpu.VMEM((2, breadth // 128, (c1 + 1) * height, 128), F32),
             pltpu.VMEM((2, c1 * height, breadth), BF16),
         ],
         cost_estimate=pl.CostEstimate(flops=2 * c1 * depth * height * breadth * 3 * mx, bytes_accessed=8 << 20, transcendentals=0),
@@ -387,7 +388,7 @@
         scratch_shapes=[
             pltpu.VMEM((c1, 8, breadth), F32),
             pltpu.VMEM((dx, c3), BF16),
-            pltpu.VMEM((4, c1 * 8, 128), F32),
+            pltpu.VMEM((4, (c1 + 1) * 8, 128), F32),
         ],
         compiler_params=pltpu.CompilerParams(vmem_limit_bytes=16 * 1024 * 1024),
     )(vol, cot, z_pair, z_cross)
@@ -397,7 +398,7 @@
     share = c3 // n_gy
     per = 448 // (2 * n_pl)
     chunk = (n_gy + 1) * per
-    rim_z, act, slope, pairs_above, back, deep, mid = pl.pallas_call(
+    rim_z, act, slope, pairs_above, back, deep, mid, turned_km = pl.pallas_call(
         functools.partial(early_kernel, (c1, c2, c3, depth, height, breadth)),
         out_shape=(
             jax.ShapeDtypeStruct(((height + 1) * blk, mx), BF16),
@@ -407,13 +408,14 @@
             back_shape,
             jax.ShapeDtypeStruct((9, c2, 3 * c3), F32),
             jax.ShapeDtypeStruct((3, 3 * blk, c2), F32),
+            jax.ShapeDtypeStruct((c2, 27 * c1), BF16),
         ),
         in_specs=[in_vmem] * 8,
-        out_specs=(in_vmem,) * 7,
+        out_specs=(in_vmem,) * 8,
         scratch_shapes=[
             pltpu.VMEM((c1 * height, breadth), BF16),
             pltpu.VMEM((dy, dx, c3), BF16),
-            pltpu.VMEM((breadth // 128, c1 * height, 128), F32),
+            pltpu.VMEM((breadth // 128, (c1 + 1) * height, 128), F32),
             pltpu.VMEM((c1 * height, breadth), BF16),
             pltpu.VMEM((my - 2, c2, mz * mx), BF16),
         ],
@@ -432,12 +434,12 @@
             pltpu.VMEM((blk, mz * mx), BF16),
             pltpu.VMEM((blk, mz * mx), BF16),
             pltpu.VMEM(((dz + 1) * mx, 3 * c3), BF16),
-            pltpu.VMEM((4 * c2, dz * dy * mx), F32),
+            pltpu.VMEM((mz, c2, mx), F32),
             pltpu.VMEM((2, c2, mz * mx), BF16),
             pltpu.VMEM((2, n_pl * chunk, 128), F32),
         ],
         compiler_params=pltpu.CompilerParams(vmem_limit_bytes=32 * 1024 * 1024),
-    )(even, odd, rim_z, act, slope, pairs, pairs_above, back, deep, mid, y_cross, y_pair, km, kd)
+    )(even, odd, rim_z, act, slope, pairs, pairs_above, back, deep, mid, y_cross, y_pair, turned_km, kd)
     other = lax.ppermute(send, "core", [(0, 1), (1, 0)])
     pair = (keep + other).astype(BF16).reshape(n_pl, chunk, 128)
     own = jnp.sum(lax.all_to_all(pair, ("dp", "gx"), 0, 0).astype(F32), axis=0)

time: 53.2 us -> 53.1 us (level)
  no operation moved by 1% of the time
where the time goes in v6:
time: 53.1 us; the launch traced here: 52.9 us
  blocking collectives  26.9 us (51%)
  starting transfers between devices  10.2 us (19%)
  Pallas kernels  10 us (19%)
  waiting for transfers between devices  1.98 us (4%)
  local copies, waits for them, and re-layouts  1.62 us (3%)
  other arithmetic  1.29 us (2%)
  between operations  0.8 us (2%)
    ppermute x4, starting transfers between devices, swapped(): return lax.ppermute(block, axis, route + [(j, i) for i, j in route])  10.1 us
    all_to_all x1, blocking collectives, on_device(): own = jnp.sum(lax.all_to_all(pair, ('dp', 'gx'), 0, 0).astype(F32), axis=0)  9.79 us
    all_gather x1, blocking collectives, on_device(): whole = lax.all_gather(own, ('dp', 'gx', 'core'), axis=0)  8.84 us
    all_to_all x1, blocking collectives, on_device(): own = jnp.sum(lax.all_to_all(column, 'gy', 0, 0).astype(F32), axis=0)  8.29 us
    pallas_call x1, Pallas kernels, on_device(): pl.pallas_call(functools.partial(early_kernel, (c1, c2, c3, depth, height...  4.18 us
    pallas_call x1, Pallas kernels, on_device(): pl.pallas_call(functools.partial(gather_kernel, (c1, depth, height, bread...  2.09 us
    ppermute x1, waiting for transfers between devices, on_device(): other = lax.ppermute(send, 'core', [(0, 1), (1, 0)])  1.97 us
    pallas_call x1, Pallas kernels, on_device(): pl.pallas_call(functools.partial(main_kernel, (c1, c2, c3, depth, height,...  1.83 us
  transfers between devices with their start and end apart: 5, of which 1 were waited for; matrix products, arithmetic and copies ran while one was open for 0% of the time, Pallas kernels for 13%

profile of v6, /device:TPU:0, one launch (start us, length us, event | category | flops | bytes accessed | tf_op | source)
XLA Modules:
  0.0 52.9 jit_solution(12394394554688031621)
XLA Ops:
  0.6 0.0 copy-start.2
  0.6 0.0 copy-start
  0.7 1.2 %pad_select_fusion = (bf16[32,16,256]{2,1,0:T(8,128)(2,1)S(1)}, bf16[32,16,256]{2,1,0:T(8,128)(2,1)S(1)}) fusion(bf16[32,16,128]{2,1,0:T(8,128)(2,1)} %bitcast.29, pred[]{:T(512)S(6)} %eq.3, bf16[32,128,256]{2,1,0:T(8,128)(2,1)} %bitcast.25), kind=kLoop, calls=%fused_computation.2 | loop fusion | flops 262144 | bytes 917505 | tf_op jit(solution)/shard_map/jit(_where)/select_n | solution.py:354
  1.8 0.7 %collective-permute-start.1 = (bf16[32,16,256]{2,1,0:T(8,128)(2,1)S(1)}, bf16[32,16,256]{2,1,0:T(8,128)(2,1)S(1)}, u32[]{:S(2)}, u32[]{:S(2)}) collective-permute-start(bf16[32,16,256]{2,1,0:T(8,128)(2,1)S(1)} %get-tuple-element.50), channel_id=1, source_target_pairs={{4,8},{8,4},{5,9},{9,5},{6,10},{10,6},{7,11},{11,7},{20,24},{24,20... | collective-permute-start | bytes 786440 | tf_op jit(solution)/shard_map/ppermute | solution.py:24
  2.5 4.3 %collective-permute-start = (bf16[32,16,256]{2,1,0:T(8,128)(2,1)S(1)}, bf16[32,16,256]{2,1,0:T(8,128)(2,1)S(1)}, u32[]{:S(2)}, u32[]{:S(2)}) collective-permute-start(bf16[32,16,256]{2,1,0:T(8,128)(2,1)S(1)} %get-tuple-element.51), channel_id=1, source_target_pairs={{0,4},{8,12},{4,0},{12,8},{1,5},{9,13},{5,1},{13,9},{2,6},{10,14},... | collective-permute-start | bytes 786440 | tf_op jit(solution)/shard_map/ppermute | solution.py:24
  6.9 0.0 copy-start.1
  6.9 1.6 %copy-done.1 = bf16[1,32,8,16,256]{4,3,2,1,0:T(8,128)(2,1)S(1)} copy-done((bf16[1,32,8,16,256]{4,3,2,1,0:T(8,128)(2,1)S(1)}, bf16[1,32,8,16,256]{4,3,2,1,0:T(8,128)(2,1)}, u32[]{:S(2)}) %copy-start.1) | copy-done | bytes 2097176
  8.4 2.1 %shard_map.60 = (bf16[1536,512]{1,0:T(8,128)(2,1)S(1)}, bf16[1536,512]{1,0:T(8,128)(2,1)S(1)}) custom-call(bf16[32,8,16,256]{3,2,1,0:T(8,128)(2,1)S(1)} %bitcast.26), custom_call_target="tpu_custom_call" | custom-call | flops 805306368 | bytes 8388608 | tf_op jit(solution)/shard_map/pallas_call | solution.py:362
  10.5 0.0 copy-done.2
  10.6 0.0 copy-done
  10.6 0.0 copy-start.3
  10.6 0.6 %shard_map.61 = (bf16[1024,384]{1,0:T(8,128)(2,1)S(1)}, f32[256,1024]{1,0:T(8,128)S(1)}) custom-call(bf16[2,4,64,128]{3,2,1,0:T(8,128)(2,1)S(1)} %bitcast.30, bf16[27,64,128]{2,1,0:T(8,128)(2,1)S(1)} %bitcast.22, bf16[1536,512]{1,0:T(8,128)(2,1)S(1)} %get-tuple-element.33.order.odd), custom_call_target="tpu_custom_call" | custom-call | flops 226492416 | bytes 2097152 | tf_op jit(solution)/shard_map/pallas_call | solution.py:374
  11.2 0.0 collective-permute-done.1.z_cross
  11.2 0.0 collective-permute-done.z_pair
  11.2 0.3 shard_map.59
  11.5 0.7 %collective-permute-start.2 = (bf16[288,256]{1,0:T(8,128)(2,1)S(1)}, bf16[288,256]{1,0:T(8,128)(2,1)S(1)}, u32[]{:S(2)}, u32[]{:S(2)}) collective-permute-start(bf16[288,256]{1,0:T(8,128)(2,1)S(1)} %get-tuple-element.43), channel_id=1, source_target_pairs={{1,2},{2,1},{5,6},{6,5},{9,10},{10,9},{13,14},{14,13},{17,18},{18,... | collective-permute-start | bytes 442376 | tf_op jit(solution)/shard_map/ppermute | solution.py:24
  12.2 4.4 %collective-permute-start.3 = (bf16[288,256]{1,0:T(8,128)(2,1)S(1)}, bf16[288,256]{1,0:T(8,128)(2,1)S(1)}, u32[]{:S(2)}, u32[]{:S(2)}) collective-permute-start(bf16[288,256]{1,0:T(8,128)(2,1)S(1)} %get-tuple-element.44), channel_id=1, source_target_pairs={{0,1},{2,3},{1,0},{3,2},{4,5},{6,7},{5,4},{7,6},{8,9},{10,11},{9,8... | collective-permute-start | bytes 442376 | tf_op jit(solution)/shard_map/ppermute | solution.py:24
  16.6 0.0 copy-done.3
  16.6 4.2 %shard_map.62 = (bf16[1632,128]{1,0:T(8,128)(2,1)S(1)}, bf16[256,1024]{1,0:T(8,128)(2,1)S(1)}, f32[8,64,512]{2,1,0:T(8,128)S(1)}, bf16[512,384]{1,0:T(8,128)(2,1...) custom-call(bf16[1536,512]{1,0:T(8,128)(2,1)S(1)} %get-tuple-element, ...), custom_call_target="tpu_custom_call" | custom-call | flops 805306368 | bytes 8388608 | tf_op jit(solution)/shard_map/pallas_call | solution.py:401
  20.8 0.0 collective-permute-done.2.y_cross
  20.8 0.0 collective-permute-done.3.y_pair
  20.8 1.8 %shard_map.63 = (f32[1120,128]{1,0:T(8,128)S(1)}, f32[1120,128]{1,0:T(8,128)S(1)}) custom-call(bf16[1536,512]{1,0:T(8,128)(2,1)S(1)} %get-tuple-element.32.even, bf16[1536,512]{1,0:T(8,128)(2,1)S(1)} %get-tuple-element.33.order.odd, bf16[1632,128]{1,0:T(8,128)(2,1)S(1)} %get-tuple-element.36.rim_z, bf16[256,1024]{1,0:T(8,128)(2,1)S(1)} %get-tuple-element.37.act, ...), custom_call_target="tpu_custom_call" | custom-call | tf_op jit(solution)/shard_map/pallas_call | solution.py:425
  22.7 0.1 collective-permute-start.4
  22.7 2.0 %collective-permute-done.4 = f32[1120,128]{1,0:T(8,128)S(1)} collective-permute-done((f32[1120,128]{1,0:T(8,128)S(1)}, f32[1120,128]{1,0:T(8,128)S(1)}, u32[]{:S(2)}, u32[]{:S(2)}) %collective-permute-start.4) | collective-permute-done | bytes 573472 | tf_op jit(solution)/shard_map/ppermute | solution.py:443
  24.7 0.1 add_convert_fusion
  24.8 9.8 %all_to_all.10 = bf16[4,280,128]{2,1,0:T(8,128)(2,1)S(1)} all-to-all(bf16[4,280,128]{2,1,0:T(8,128)(2,1)S(1)} %bitcast.33), channel_id=1, replica_groups=mesh['dp'=2,'gx'=2,'core'=2,'gy'=4] {'dp','gx'}, dimensions={0} | all-to-all | bytes 573440 | tf_op jit(solution)/shard_map/all_to_all | solution.py:445
  34.7 8.3 %all_to_all.11 = bf16[4,112,128]{2,1,0:T(8,128)(2,1)S(1)} all-to-all(bf16[4,112,128]{2,1,0:T(8,128)(2,1)S(1)} %pad_maximum_fusion), channel_id=1, replica_groups=mesh['dp'=2,'gx'=2,'core'=2,'gy'=4] {'gy'}, dimensions={0} | all-to-all | bytes 229376 | tf_op jit(solution)/shard_map/all_to_all | solution.py:449
  43.0 8.8 %all-gather = f32[896,128]{1,0:T(8,128)S(1)} all-gather(f32[112,128]{1,0:T(8,128)S(1)} %convert_reduce_fusion.1), channel_id=2, replica_groups=mesh['dp'=2,'gx'=2,'core'=2,'gy'=4] {'dp','gx','core'}, dimensions={0}, use_global_device_ids=true | all-gather | bytes 516096 | tf_op jit(solution)/shard_map/all_gather | solution.py:450
  51.8 1.0 %shard_map.64 = (f32[864,64]{1,0:T(8,128)}, f32[27,32,64]{2,1,0:T(8,128)}) custom-call(f32[8,112,128]{2,1,0:T(8,128)S(1)} %bitcast.28), custom_call_target="tpu_custom_call" | custom-call | tf_op jit(solution)/shard_map/pallas_call | solution.py:452
  (6 shorter events, 0.1 us)
Async XLA Ops:
  0.6 9.9 %copy-start.2 = (bf16[1,128,2,4,64]{1,4,3,2,0:T(8,128)(2,1)S(1)}, bf16[1,128,2,4,64]{1,4,3,2,0:T(8,128)(2,1)}, u32[]{:S(2)}) copy-start(bf16[1,128,2,4,64]{1,4,3,2,0:T(8,128)(2,1)} %param.7) | copy-start | bytes 393220
  0.6 9.9 %copy-start = (bf16[128,64,3,3,3]{0,1,4,3,2:T(8,128)(2,1)S(1)}, bf16[128,64,3,3,3]{0,1,4,3,2:T(8,128)(2,1)}, u32[]{:S(2)}) copy-start(bf16[128,64,3,3,3]{0,1,4,3,2:T(8,128)(2,1)} %param.6) | copy-start | bytes 1327108
  1.8 9.4 %collective-permute-start.1 = (bf16[32,16,256]{2,1,0:T(8,128)(2,1)S(1)}, bf16[32,16,256]{2,1,0:T(8,128)(2,1)S(1)}, u32[]{:S(2)}, u32[]{:S(2)}) collective-permute-start(bf16[32,16,256]{2,1,0:T(8,128)(2,1)S(1)} %get-tuple-element.50), channel_id=1, source_target_pairs={{4,8},{8,4},{5,9},{9,5},{6,10},{10,6},{7,11},{11,7},{20,24},{24,20... | collective-permute-start | bytes 786440 | tf_op jit(solution)/shard_map/ppermute | solution.py:24
  2.5 8.7 %collective-permute-start = (bf16[32,16,256]{2,1,0:T(8,128)(2,1)S(1)}, bf16[32,16,256]{2,1,0:T(8,128)(2,1)S(1)}, u32[]{:S(2)}, u32[]{:S(2)}) collective-permute-start(bf16[32,16,256]{2,1,0:T(8,128)(2,1)S(1)} %get-tuple-element.51), channel_id=1, source_target_pairs={{0,4},{8,12},{4,0},{12,8},{1,5},{9,13},{5,1},{13,9},{2,6},{10,14},... | collective-permute-start | bytes 786440 | tf_op jit(solution)/shard_map/ppermute | solution.py:24
  6.9 1.6 %copy-start.1 = (bf16[1,32,8,16,256]{4,3,2,1,0:T(8,128)(2,1)S(1)}, bf16[1,32,8,16,256]{4,3,2,1,0:T(8,128)(2,1)}, u32[]{:S(2)}) copy-start(bf16[1,32,8,16,256]{4,3,2,1,0:T(8,128)(2,1)} %param.4) | copy-start | bytes 6291460
  10.6 6.1 %copy-start.3 = (bf16[64,32,3,3,3]{0,1,4,3,2:T(8,128)(2,1)S(1)}, bf16[64,32,3,3,3]{0,1,4,3,2:T(8,128)(2,1)}, u32[]{:S(2)}) copy-start(bf16[64,32,3,3,3]{0,1,4,3,2:T(8,128)(2,1)} %param.5) | copy-start | bytes 331780
  11.5 9.3 %collective-permute-start.2 = (bf16[288,256]{1,0:T(8,128)(2,1)S(1)}, bf16[288,256]{1,0:T(8,128)(2,1)S(1)}, u32[]{:S(2)}, u32[]{:S(2)}) collective-permute-start(bf16[288,256]{1,0:T(8,128)(2,1)S(1)} %get-tuple-element.43), channel_id=1, source_target_pairs={{1,2},{2,1},{5,6},{6,5},{9,10},{10,9},{13,14},{14,13},{17,18},{18,... | collective-permute-start | bytes 442376 | tf_op jit(solution)/shard_map/ppermute | solution.py:24
  12.2 8.7 %collective-permute-start.3 = (bf16[288,256]{1,0:T(8,128)(2,1)S(1)}, bf16[288,256]{1,0:T(8,128)(2,1)S(1)}, u32[]{:S(2)}, u32[]{:S(2)}) collective-permute-start(bf16[288,256]{1,0:T(8,128)(2,1)S(1)} %get-tuple-element.44), channel_id=1, source_target_pairs={{0,1},{2,3},{1,0},{3,2},{4,5},{6,7},{5,4},{7,6},{8,9},{10,11},{9,8... | collective-permute-start | bytes 442376 | tf_op jit(solution)/shard_map/ppermute | solution.py:24
  22.7 2.0 %collective-permute-start.4 = (f32[1120,128]{1,0:T(8,128)S(1)}, f32[1120,128]{1,0:T(8,128)S(1)}, u32[]{:S(2)}, u32[]{:S(2)}) collective-permute-start(f32[1120,128]{1,0:T(8,128)S(1)} %get-tuple-element.47), channel_id=1, source_target_pairs={{0,4},{4,0},{1,5},{5,1},{2,6},{6,2},{3,7},{7,3},{8,12},{12,8},{9,1... | collective-permute-start | bytes 1720328 | tf_op jit(solution)/shard_map/ppermute | solution.py:443
